TPU v7x, 512 devices: a whole 4x8x8 slice. The times are simulated.
512 devices in a mesh: slab: 8 (over z_hi, core), dom: 64 (over y, x, z_lo).
Axes of the slice: x: 4, y: 8, z: 8 (z_hi: 4, z_lo: 2; z = z_hi * 2 + z_lo), core: 2. Of those that a mesh axis runs over, the one named last changes fastest.
Arguments:
- particles: bfloat16 [2048, 256, 2, 128], P(('slab', 'dom')), may hold values from -6 to 6
- defocus: float32 [2048], P(('slab', 'dom')), may hold values from 8000 to 30000
- inverse_noise: float32 [2048], P(('slab', 'dom')), may hold values from 0.002 to 0.05
- volume: bfloat16 [2, 33554432], P(None, ('slab', 'dom')), may hold values from -6 to 6
- slice_owner: int32 [8, 256], replicated, may hold values from 0 to 511, as said below
- slice_voxel: int32 [8, 256, 128], replicated, may hold values from 0 to 65535
Outputs:
- back_projection: float32 [2, 33554432], P(None, ('slab', 'dom'))
Inputs may be any that keep to these rules, and one draw needn't show every extreme that they name: `slice_owner`: no device owns more than 6 slice rows, and some device owns exactly 6.
All inputs are finite; a program needn't handle non-finite values.
Results may differ from a plain program's by a relative error of at most 0.005.
Values may be sent and summed in bfloat16 or wider, within the bound.
No kernel may reach another device: no remote copies, remote signals or barrier semaphores. Data moves between devices by JAX's collectives and lax.ppermute only.
A program may use at most 128 MiB of HBM per device.

v0:
```python
import math

import jax
import jax.numpy as jnp
from jax import lax
from jax.sharding import PartitionSpec as P

SHIFTS = 32


box_edge = 400
wavelength = 0.0197
amp_contrast = 0.1


def contrast_transfer(defocus_value, ky_count, kx_count):
    freq_y = (jnp.arange(ky_count, dtype=jnp.int32) - ky_count // 2).astype(jnp.float32)
    freq_x = jnp.arange(kx_count, dtype=jnp.int32).astype(jnp.float32)
    radius_sq = (freq_y[:, None] * freq_y[:, None] + freq_x[None, :] * freq_x[None, :]) / (
        box_edge * box_edge
    )
    chi_angle = math.pi * wavelength * defocus_value * radius_sq
    return -(math.sqrt(0.99) * jnp.sin(chi_angle) + amp_contrast * jnp.cos(chi_angle))


def phase_tables(ky_count, kx_count, shift_count):
    shift_vals = jnp.arange(shift_count, dtype=jnp.int32) - shift_count // 2
    freq_y = jnp.arange(ky_count, dtype=jnp.int32) - ky_count // 2
    freq_x = jnp.arange(kx_count, dtype=jnp.int32)
    angle_y = (
        2.0
        * math.pi
        / box_edge
        * jnp.mod(freq_y[:, None] * shift_vals[None, :], box_edge).astype(jnp.float32)
    )
    angle_x = (
        2.0
        * math.pi
        / box_edge
        * jnp.mod(freq_x[:, None] * shift_vals[None, :], box_edge).astype(jnp.float32)
    )
    cos_y = jnp.cos(angle_y).astype(jnp.bfloat16)
    sin_y = jnp.sin(angle_y).astype(jnp.bfloat16)
    cos_x = jnp.cos(angle_x).astype(jnp.bfloat16)
    sin_x = jnp.sin(angle_x).astype(jnp.bfloat16)
    forward_x = jnp.concatenate(
        [jnp.concatenate([cos_x, sin_x], axis=1), jnp.concatenate([-sin_x, cos_x], axis=1)], axis=0
    )
    backward_x = jnp.concatenate(
        [jnp.concatenate([cos_x.T, sin_x.T], axis=1), jnp.concatenate([-sin_x.T, cos_x.T], axis=1)],
        axis=0,
    )
    corr_y = jnp.concatenate([cos_y.T, -sin_y.T], axis=1)
    back_y = jnp.concatenate([cos_y, sin_y], axis=0)
    return (forward_x, backward_x, corr_y, back_y)


def particle_term(image, defocus_value, noise_scale, slices, tables):
    forward_x, backward_x, corr_y, back_y = tables
    ref_count, ky_count, _, kx_count = slices.shape
    shift_count = corr_y.shape[0]
    ctf_values = contrast_transfer(defocus_value, ky_count, kx_count)
    image_f = image.astype(jnp.float32)
    image_re = image_f[:, 0, :]
    image_im = image_f[:, 1, :]
    slice_re = slices[:, :, 0, :].astype(jnp.float32)
    slice_im = slices[:, :, 1, :].astype(jnp.float32)
    q_re = ctf_values * (slice_re * image_re + slice_im * image_im)
    q_im = ctf_values * (slice_re * image_im - slice_im * image_re)
    q_all = jnp.stack([q_re, q_im], axis=2).astype(jnp.bfloat16)
    row_phase = jnp.dot(
        q_all.reshape(ref_count * ky_count, 2 * kx_count),
        forward_x,
        preferred_element_type=jnp.float32,
    )
    row_phase = row_phase.astype(jnp.bfloat16).reshape(ref_count, ky_count, 2, shift_count)
    row_phase = jnp.transpose(row_phase, (0, 2, 1, 3)).reshape(ref_count, 2 * ky_count, shift_count)
    corr = jnp.einsum("ik,rkj->rij", corr_y, row_phase, preferred_element_type=jnp.float32)
    power = jnp.sum(
        (ctf_values * ctf_values)[None] * (slice_re * slice_re + slice_im * slice_im), axis=(1, 2)
    )
    score = noise_scale * (corr - 0.5 * power[:, None, None])
    weight = jax.nn.softmax(score.reshape(-1)).reshape(score.shape).astype(jnp.bfloat16)
    col_phase = jnp.einsum(
        "ki,rij->rkj", back_y, weight, preferred_element_type=jnp.float32
    ).astype(jnp.bfloat16)
    col_phase = jnp.transpose(col_phase.reshape(ref_count, 2, ky_count, shift_count), (0, 2, 1, 3))
    shift_sum = jnp.dot(
        col_phase.reshape(ref_count * ky_count, 2 * shift_count),
        backward_x,
        preferred_element_type=jnp.float32,
    )
    shift_sum = shift_sum.astype(jnp.bfloat16).reshape(ref_count, ky_count, 2, kx_count)
    sum_re = shift_sum[:, :, 0, :].astype(jnp.float32)
    sum_im = shift_sum[:, :, 1, :].astype(jnp.float32)
    term_re = ctf_values * (image_re * sum_re - image_im * sum_im)
    term_im = ctf_values * (image_re * sum_im + image_im * sum_re)
    return jnp.stack([term_re, term_im], axis=2)


def slot_tables(owner_flat, device_count, capacity, my_index):
    row_count = owner_flat.shape[0]
    owner_hits = (owner_flat[:, None] == jnp.arange(device_count, dtype=jnp.int32)[None, :]).astype(
        jnp.int32
    )
    slot_of_row = jnp.sum((jnp.cumsum(owner_hits, axis=0) - 1) * owner_hits, axis=1)
    owner_counts = jnp.sum(owner_hits, axis=0)
    is_mine = (owner_flat == my_index)[:, None] & (
        slot_of_row[:, None] == jnp.arange(capacity, dtype=jnp.int32)[None, :]
    )
    row_ids = jnp.arange(row_count, dtype=jnp.int32)
    my_rows = jnp.sum(jnp.where(is_mine, row_ids[:, None], 0), axis=0)
    filled = jnp.any(is_mine, axis=0)
    return (slot_of_row, owner_counts, my_rows, filled)


def local(particles, defocus, inverse_noise, volume, slice_owner, slice_voxel):
    device_count = lax.axis_size(("slab", "dom"))
    my_index = lax.axis_index(("slab", "dom"))
    ref_count, ky_count = slice_owner.shape
    kx_count = slice_voxel.shape[2]
    row_count = ref_count * ky_count
    capacity = max(2, 3 * row_count // (2 * device_count))
    owner_flat = slice_owner.reshape(row_count)
    voxel_rows = slice_voxel.reshape(row_count, kx_count)
    slot_of_row, owner_counts, my_rows, filled = slot_tables(
        owner_flat, device_count, capacity, my_index
    )
    own_voxels = voxel_rows[my_rows]
    picked = jnp.stack([volume[0][own_voxels], volume[1][own_voxels]], axis=1)
    compact = jnp.where(filled[:, None, None], picked, jnp.zeros_like(picked))
    everyone = lax.all_gather(compact, ("slab", "dom"), axis=0, tiled=True)
    slices = everyone[owner_flat * capacity + slot_of_row]
    slices = slices.reshape(ref_count, ky_count, 2, kx_count)
    tables = phase_tables(ky_count, kx_count, SHIFTS)

    def accumulate(total, item):
        image, defocus_value, noise_scale = item
        return (total + particle_term(image, defocus_value, noise_scale, slices, tables), None)

    start = jnp.zeros((ref_count, ky_count, 2, kx_count), jnp.float32)
    inserted, _ = lax.scan(accumulate, start, (particles, defocus, inverse_noise))
    flat_inserted = inserted.reshape(row_count, 2, kx_count)
    summed = lax.psum(flat_inserted, ("slab", "dom"))
    received = summed[my_rows]
    received = jnp.where(filled[:, None, None], received, 0.0)
    particle_total = particles.shape[0] * device_count
    added = jnp.zeros(volume.shape, jnp.float32).at[:, own_voxels].add(jnp.moveaxis(received, 1, 0))
    return added / math.sqrt(particle_total)


def solution(mesh):
    in_specs = (
        P(("slab", "dom"), None, None, None),
        P(("slab", "dom")),
        P(("slab", "dom")),
        P(None, ("slab", "dom")),
        P(),
        P(),
    )
    out_specs = P(None, ("slab", "dom"))
    return jax.shard_map(local, mesh=mesh, in_specs=in_specs, out_specs=out_specs, check_vma=False)
```

profile of v0, /device:TPU:1, one launch (start us, length us, event | category | flops | bytes accessed | tf_op | source)
XLA Modules:
  0.0 1490.2 jit_solution(17500367206713689804)
XLA Ops:
  8.6 1.9 copy-done.4
  10.6 2.7 add_add_fusion
  13.4 4.4 copy.66
  17.7 2.7 fusion.26
  20.8 1.4 slice_reduce_fusion.1
  22.8 5.0 gather_fusion.2
  27.8 5.0 gather_fusion.1
  37.7 1049.0 %all-gather.2.cloned.1.call-done = bf16[3072,2,128]{2,1,0:T(2,128)(2,1)} async-done(((bf16[6,2,128]{2,1,0:T(2,128)(2,1)}), bf16[3072,2,128]{2,1,0:T(2,128)(2,1)}) %all-gather.2.cloned.1.call-update) | async-done | bytes 1572880 | tf_op jit(solution)/shard_map/all_gather | solution.py:132
  1086.7 8.5 gather_fusion.3
  1095.4 64.8 %while.13 = (s32[]{:T(128)}, f32[8,256,2,128]{3,1,2,0:T(8,128)}, f32[4]{0:T(128)S(1)}, bf16[4,256,2,128]{3,2,1,0:T(2,128)(2,1)}, f32[4]{0:T(128)S(1)}, /*index=5...) while((s32[]{:T(128)}, f32[8,256,2,128]{3,1,2,0:T(8,128)}, ...), condition=%wide.region_9.10_spmd.clone, body=%wide.region_5.9_spmd.clone.sunk | while | flops 161842176 | bytes 49122980 | solution.py:142
  1097.2 1.0 constant_dynamic-slice_fusion.2
  1099.6 0.9 copy.105
  1100.9 1.2 convolution_convert_fusion.5
  1102.6 1.3 fusion.91
  1104.0 1.2 fusion.92
  1105.2 1.4 fusion.93
  1107.6 1.5 fusion.94
  1110.2 1.3 copy-done.3
  1113.4 1.0 constant_dynamic-slice_fusion.2
  1115.8 0.9 copy.105
  1117.1 1.2 convolution_convert_fusion.5
  1118.8 1.4 fusion.91
  1120.2 1.2 fusion.92
  1121.4 1.4 fusion.93
  1123.8 1.5 fusion.94
  1126.4 1.3 copy-done.3
  1129.6 1.0 constant_dynamic-slice_fusion.2
  1132.1 0.9 copy.105
  1133.3 1.2 convolution_convert_fusion.5
  1135.0 1.4 fusion.91
  1136.4 1.2 fusion.92
  1137.6 1.4 fusion.93
  1140.0 1.5 fusion.94
  1142.6 1.3 copy-done.3
  1145.8 1.0 constant_dynamic-slice_fusion.2
  1148.3 0.9 copy.105
  1149.5 1.2 convolution_convert_fusion.5
  1151.2 1.4 fusion.91
  1152.6 1.2 fusion.92
  1153.8 1.4 fusion.93
  1156.3 1.5 fusion.94
  1158.9 1.3 copy-done.3
  1160.2 4.5 copy.72
  1164.7 277.9 %all-reduce.2.cloned.1.call-done = f32[2048,2,128]{2,1,0:T(2,128)} async-done(((f32[2048,2,128]{2,1,0:T(2,128)}), f32[2048,2,128]{2,1,0:T(2,128)}) %all-reduce.2.cloned.1.call-update) | async-done | bytes 2097168 | tf_op jit(solution)/shard_map/psum | solution.py:144
  1442.7 2.2 gather_fusion.4
  1445.1 19.4 %scatter_custom_fusion = f32[2,65536]{0,1:T(8,128)} fusion(s32[768]{0:T(1024)S(1)} %fusion.53, f32[768,2]{1,0:T(8,128)S(1)} %copy.73, f32[]{:T(128)} %constant.106.clone.1), kind=kCustom, calls=%fused_computation.56 | custom fusion | flops 1536 | bytes 524292 | tf_op jit(solution)/shard_map/scatter-add | solution.py:148
  1464.5 17.8 %copy.74 = f32[2,65536]{1,0:T(2,128)S(1)} copy(f32[2,65536]{0,1:T(8,128)} %scatter_custom_fusion) | data formatting | bytes 1048576 | tf_op jit(solution)/shard_map/scatter-add | solution.py:148
  1482.3 1.1 broadcast_multiply_fusion.1
  (197 shorter events, 30.2 us)
Async XLA Ops:
  6.5 15.6 %copy-start = (s32[8,256,128]{2,1,0:T(8,128)S(1)}, s32[8,256,128]{2,1,0:T(8,128)}, u32[]{:S(2)}) copy-start(s32[8,256,128]{2,1,0:T(8,128)} %param.13) | copy-start | bytes 3145732
  6.5 1080.1 %all-gather.2.cloned.1.call-start = ((), (), s32[]{:S(2)}) async-start(), calls=%async_computation | async-start | bytes 1575936 | tf_op jit(solution)/shard_map/all_gather | solution.py:132
  8.6 1.9 copy-start.4
  17.7 3.0 copy-start.7
  17.7 16.0 %copy-start.8 = (s32[8,256]{1,0:T(8,128)S(1)}, s32[8,256]{1,0:T(8,128)}, u32[]{:S(2)}) copy-start(s32[8,256]{1,0:T(8,128)} %param.12) | copy-start | bytes 24580
  22.8 1072.6 %copy-start.10 = (f32[4]{0:T(128)S(1)}, f32[4]{0:T(128)}, u32[]{:S(2)}) copy-start(f32[4]{0:T(128)} %param.9) | copy-start | bytes 52
  22.8 1072.6 %copy-start.12 = (f32[4]{0:T(128)S(1)}, f32[4]{0:T(128)}, u32[]{:S(2)}) copy-start(f32[4]{0:T(128)} %param.10) | copy-start | bytes 52
  33.5 1409.2 %all-reduce.2.cloned.1.call-start = ((), (), s32[]{:S(2)}) async-start(), calls=%async_computation.1 | async-start | bytes 4194304 | tf_op jit(solution)/shard_map/psum | solution.py:144
  1100.6 2.0 copy-start.5
  1100.6 4.6 copy-start.9
  1100.9 6.0 copy-start.6
  1107.6 1.9 copy-start.2
  1109.5 2.1 copy-start.11
  1109.5 2.1 copy-start.13
  1110.2 1.4 copy-start.3
  1116.8 2.0 copy-start.5
  1116.8 4.6 copy-start.9
  1117.1 6.0 copy-start.6
  1123.8 1.9 copy-start.2
  1125.7 2.1 copy-start.11
  1125.7 2.1 copy-start.13
  1126.4 1.4 copy-start.3
  1133.0 2.0 copy-start.5
  1133.0 4.6 copy-start.9
  1133.3 6.0 copy-start.6
  1140.0 1.9 copy-start.2
  1141.9 2.1 copy-start.11
  1141.9 2.1 copy-start.13
  1142.6 1.4 copy-start.3
  1149.2 2.0 copy-start.5
  1149.2 4.6 copy-start.9
  1149.5 6.0 copy-start.6
  1156.2 1.9 copy-start.2
  1158.1 2.1 copy-start.11
  1158.1 2.1 copy-start.13
  1158.8 1.4 copy-start.3
  1464.5 18.8 %copy-start.1 = (s32[8,256,128]{2,1,0:T(8,128)S(1)}, s32[8,256,128]{2,1,0:T(8,128)}, u32[]{:S(2)}) copy-start(s32[8,256,128]{2,1,0:T(8,128)} %param.13) | copy-start | bytes 3145732
Sparse Core Ops, SparseCore 0:
  33.6 1052.9 all-gather.1
  1164.8 277.7 all-reduce.1
where the time goes:
time: 1490 us
  waiting for transfers between devices  1330 us (89%)
  local copies, waits for them, and re-layouts  83 us (6%)
  other arithmetic  45.4 us (3%)
  matrix products  17.4 us (1%)
    all_gather x1, waiting for transfers between devices, local(): everyone = lax.all_gather(compact, ('slab', 'dom'), axis=0, tiled=True)  1050 us
    psum x1, waiting for transfers between devices, local(): summed = lax.psum(flat_inserted, ('slab', 'dom'))  278 us
  transfers between devices with their start and end apart: 2, of which 2 were waited for; matrix products, arithmetic and copies ran while one was open for 0% of the time, Pallas kernels for 0%

commit v1 on v0

v1 whole, which is shorter than its diff:
```python
import math

import jax
import jax.numpy as jnp
import ml_dtypes
import numpy as np
from jax import lax
from jax.experimental import pallas as pl
from jax.experimental.pallas import tpu as pltpu
from jax.sharding import Mesh
from jax.sharding import PartitionSpec as P

KY, KX, REFS, SHIFTS, CAP, PER = 256, 128, 8, 32, 6, 4
ROWS = REFS * KY
PARTICLES = 2048
HALF = 1536
BOX = 400
WAVE = 0.0197
AMP = 0.1
VMEM_LIMIT = 40 * 1024 * 1024
FINE = ("zh", "c", "y", "x", "zl")
F32 = jnp.float32
BF16 = jnp.bfloat16


def phase_constants():
    shift = np.arange(SHIFTS) - SHIFTS // 2
    fy = np.arange(KY) - KY // 2
    fx = np.arange(KX)
    ang_y = 2.0 * np.pi / BOX * np.mod(fy[:, None] * shift[None, :], BOX)
    ang_x = 2.0 * np.pi / BOX * np.mod(fx[:, None] * shift[None, :], BOX)
    cos_y, sin_y, cos_x, sin_x = np.cos(ang_y), np.sin(ang_y), np.cos(ang_x), np.sin(ang_x)
    fwd = np.zeros((PER, 2, KX, 2, PER, SHIFTS))
    bwd = np.zeros((2, PER, SHIFTS, PER, 2, KX))
    for p in range(PER):
        fwd[p, 0, :, 0, p], fwd[p, 0, :, 1, p] = cos_x, sin_x
        fwd[p, 1, :, 0, p], fwd[p, 1, :, 1, p] = -sin_x, cos_x
        bwd[0, p, :, p, 0], bwd[0, p, :, p, 1] = cos_x.T, sin_x.T
        bwd[1, p, :, p, 0], bwd[1, p, :, p, 1] = -sin_x.T, cos_x.T
    fwd = fwd.reshape(PER * 2 * KX, 2 * PER * SHIFTS)
    bwd = bwd.reshape(2 * PER * SHIFTS, PER * 2 * KX)
    corr = np.concatenate([cos_y.T, sin_y.T], axis=0)
    back = np.concatenate([cos_y, sin_y], axis=0)
    return [a.astype(np.float32).astype(ml_dtypes.bfloat16) for a in (fwd, bwd, corr, back)]


def iota(shape, dim):
    return lax.broadcasted_iota(jnp.int32, shape, dim)


def pick_kernel(me_ref, own_ref, own_t_ref, vol_ref, vox_ref, pos_ref, mine_ref, out_ref, slot, stage):
    me = me_ref[0]
    blocks = ROWS // 128
    cols = [jnp.broadcast_to(own_t_ref[:, c : c + 1], (128, 128)) for c in range(blocks)]
    earlier = iota((128, 128), 0) < iota((128, 128), 1)
    for b in range(blocks):
        here = jnp.broadcast_to(own_ref[b : b + 1, :], (128, 128))
        hits = ((cols[b] == here) & earlier).astype(F32)
        for c in range(b):
            hits = hits + (cols[c] == here).astype(F32)
        slot[b : b + 1, :] = jnp.sum(hits, axis=0, keepdims=True).astype(jnp.int32)
    own = own_ref[...]
    slots = slot[...]
    g1 = lax.shift_right_logical(own, 7) * 2 + (own & 1)
    g2 = (lax.shift_right_logical(own, 3) & 7) * 4 + (lax.shift_right_logical(own, 1) & 3)
    across = ((lax.shift_right_logical(own, 6) ^ lax.shift_right_logical(me, 6)) & 1) * HALF
    pos_ref[...] = across + g2 * 48 + g1 * CAP + jnp.minimum(slots, CAP - 1)
    row_id = iota((blocks, 128), 0) * 128 + iota((blocks, 128), 1)
    is_me = own == me
    table = vol_ref[...]
    parity = (iota((8, 128), 0) & 1) == 0
    row_pair = lax.shift_right_logical(iota((1024, 128), 0), 1)
    lo_iota = iota((128, 128), 0)
    mine_ref[...] = jnp.full((8, 128), -1, jnp.int32)
    for k in range(CAP):
        hit = is_me & (slots == k)
        row = jnp.max(jnp.where(hit, row_id, -1))
        vox = vox_ref[pl.ds(jnp.maximum(row, 0), 1), :]
        vox = jnp.where(row >= 0, vox, -1)
        mine_ref[k : k + 1, :] = vox
        hi = lax.shift_right_arithmetic(vox, 7)
        onehot = (lo_iota == (vox & 127)).astype(F32).astype(BF16)
        wide = jnp.dot(table, onehot, preferred_element_type=F32)
        kept = jnp.where(row_pair == hi, wide, 0.0)
        kept = jnp.sum(kept.reshape(128, 8, 128), axis=0)
        re = jnp.sum(jnp.where(parity, kept, 0.0), axis=0, keepdims=True)
        im = jnp.sum(jnp.where(parity, 0.0, kept), axis=0, keepdims=True)
        for copy in range(8):
            stage[copy * 12 + 2 * k : copy * 12 + 2 * k + 1, :] = re
            stage[copy * 12 + 2 * k + 1 : copy * 12 + 2 * k + 2, :] = im
    out_ref[...] = stage[...].astype(BF16)


def image_kernel(defocus_ref, part_ref, img_ref, sq_ref, wide):
    fy = (iota((KY, KX), 0) - KY // 2).astype(F32)
    fx = iota((KY, KX), 1).astype(F32)
    radius = (fy * fy + fx * fx) / float(BOX * BOX)
    phase0 = math.asin(AMP)
    pi_a = 3.140625
    pi_b = 9.67502593994140625e-4
    pi_c = math.pi - pi_a - pi_b
    coef = [(-1.0) ** k / math.factorial(2 * k + 1) for k in range(7)]
    for p in range(PER):
        wide[...] = part_ref[p * 512 : (p + 1) * 512, :].astype(F32)
        chi = (math.pi * WAVE * defocus_ref[p]) * radius
        whole = jnp.floor(chi * (1.0 / math.pi) + (phase0 / math.pi + 0.5))
        frac = ((chi - whole * pi_a) - whole * pi_b) - (whole * pi_c - phase0)
        half = whole * 0.5
        frac = frac * (1.0 - 4.0 * (half - jnp.floor(half)))
        sq = frac * frac
        poly = jnp.full_like(sq, coef[6])
        for k in range(5, -1, -1):
            poly = poly * sq + coef[k]
        ctf = -(poly * frac)
        sq_ref[p * KY : (p + 1) * KY, :] = ctf * ctf
        img_ref[p * 512 : p * 512 + KY, :] = ctf * wide[pl.ds(0, KY, stride=2), :]
        img_ref[p * 512 + KY : (p + 1) * 512, :] = ctf * wide[pl.ds(1, KY, stride=2), :]


CH = 64


def search_kernel(pos_ref, noise_ref, near_ref, far_ref, img_ref, sq_ref, fwd_ref, bwd_ref, corr_ref, back_ref,
                  sum_ref, far_out_ref, slots, rows, q, power, corr, weight):
    slots[0 : 2 * HALF, :] = near_ref[...].astype(F32)
    slots[2 * HALF : 4 * HALF, :] = far_ref[...].astype(F32)
    sum_ref[...] = jnp.zeros_like(sum_ref)

    def forward(r, carry):
        def fetch(g, c):
            for u in range(32):
                y = g * 32 + u
                at = pl.multiple_of(2 * pos_ref[r * KY + y], 2)
                rows[pl.ds(pl.multiple_of(2 * y, 2), 2), :] = slots[pl.ds(at, 2), :]
            return c

        lax.fori_loop(0, KY // 32, fetch, 0)
        sums = [jnp.zeros((8, KX), F32) for _ in range(PER)]
        for k in range(KY // CH):
            re = rows[pl.ds(2 * CH * k, CH, stride=2), :]
            im = rows[pl.ds(2 * CH * k + 1, CH, stride=2), :]
            mag = re * re + im * im
            for p in range(PER):
                a_re = img_ref[p * 512 + k * CH : p * 512 + (k + 1) * CH, :]
                a_im = img_ref[p * 512 + KY + k * CH : p * 512 + KY + (k + 1) * CH, :]
                q[k * CH : (k + 1) * CH, p * 256 : p * 256 + 128] = (re * a_re + im * a_im).astype(BF16)
                q[k * CH : (k + 1) * CH, p * 256 + 128 : (p + 1) * 256] = (re * a_im - im * a_re).astype(BF16)
                part = sq_ref[p * KY + k * CH : p * KY + (k + 1) * CH, :] * mag
                sums[p] = sums[p] + jnp.sum(part.reshape(CH // 8, 8, KX), axis=0)
        for p in range(PER):
            power[pl.ds(p * REFS + r, 1), :] = jnp.sum(sums[p], axis=0, keepdims=True)
        row_phase = jnp.dot(q[...], fwd_ref[...], preferred_element_type=F32).astype(BF16)
        both = jnp.dot(corr_ref[...], row_phase, preferred_element_type=F32)
        corr[pl.ds(pl.multiple_of(r * SHIFTS, SHIFTS), SHIFTS), :] = both[:SHIFTS, :128] - both[SHIFTS:, 128:]
        return carry

    lax.fori_loop(0, REFS, forward, 0)

    group = lax.shift_right_logical(iota((1, 128), 1), 5)
    noise = jnp.zeros((1, 128), F32)
    totals = jnp.zeros((REFS, 128), F32)
    for p in range(PER):
        noise = jnp.where(group == p, noise_ref[p], noise)
        column = jnp.sum(power[p * REFS : (p + 1) * REFS, :], axis=1, keepdims=True)
        totals = jnp.where(group == p, column, totals)
    score = corr[...].reshape(REFS, SHIFTS, 128) - 0.5 * totals[:, None, :]
    score = score.reshape(REFS * SHIFTS, 128) * noise
    top = jnp.max(score, axis=0, keepdims=True)
    peak = jnp.zeros((1, 128), F32)
    for p in range(PER):
        peak = jnp.where(group == p, jnp.max(jnp.where(group == p, top, -jnp.inf), axis=1, keepdims=True), peak)
    expo = jnp.exp(score - peak)
    lane_sum = jnp.sum(expo, axis=0, keepdims=True)
    norm = jnp.ones((1, 128), F32)
    for p in range(PER):
        norm = jnp.where(group == p, jnp.sum(jnp.where(group == p, lane_sum, 0.0), axis=1, keepdims=True), norm)
    weight[...] = (expo * (1.0 / norm)).astype(BF16)

    def backward(r, carry):
        w = weight[pl.ds(pl.multiple_of(r * SHIFTS, SHIFTS), SHIFTS), :]
        col = jnp.dot(back_ref[...], w, preferred_element_type=F32).astype(BF16)
        col = jnp.concatenate([col[:KY], col[KY:]], axis=1)
        for k in range(KY // CH):
            ss = jnp.dot(col[k * CH : (k + 1) * CH], bwd_ref[...], preferred_element_type=F32).astype(BF16).astype(F32)
            t_re = t_im = None
            for p in range(PER):
                a_re = img_ref[p * 512 + k * CH : p * 512 + (k + 1) * CH, :]
                a_im = img_ref[p * 512 + KY + k * CH : p * 512 + KY + (k + 1) * CH, :]
                s_re = ss[:, p * 256 : p * 256 + 128]
                s_im = ss[:, p * 256 + 128 : (p + 1) * 256]
                u_re = a_re * s_re - a_im * s_im
                u_im = a_re * s_im + a_im * s_re
                t_re = u_re if t_re is None else t_re + u_re
                t_im = u_im if t_im is None else t_im + u_im
            rows[pl.ds(2 * CH * k, CH, stride=2), :] = t_re
            rows[pl.ds(2 * CH * k + 1, CH, stride=2), :] = t_im

        def put(g, c):
            for u in range(32):
                y = g * 32 + u
                at = pl.multiple_of(2 * pos_ref[r * KY + y], 2)
                sum_ref[pl.ds(at, 2), :] = rows[pl.ds(pl.multiple_of(2 * y, 2), 2), :]
            return c

        lax.fori_loop(0, KY // 32, put, 0)
        return carry

    lax.fori_loop(0, REFS, backward, 0)
    far_out_ref[...] = sum_ref[2 * HALF : 4 * HALF, :].astype(BF16)


def insert_kernel(mine_ref, got_ref, out_ref, wide, left, right):
    wide[...] = got_ref[...].astype(F32)
    scale = 1.0 / math.sqrt(PARTICLES)
    hi_iota = iota((512, 128), 0)
    lo_iota = iota((128, 128), 0)
    for k in range(CAP):
        vox = mine_ref[k : k + 1, :]
        hi = lax.shift_right_arithmetic(vox, 7)
        onehot = (lo_iota == (vox & 127)).astype(F32).astype(BF16)
        right[:, 2 * k * 128 : (2 * k + 1) * 128] = onehot
        right[:, (2 * k + 1) * 128 : (2 * k + 2) * 128] = onehot
        at = hi_iota == hi
        for c in range(2):
            total = jnp.zeros((1, 128), F32)
            for src in range(8):
                total = total + wide[src * 12 + 2 * k + c : src * 12 + 2 * k + c + 1, :]
            total = total * scale
            first = total.astype(BF16).astype(F32)
            rest = total - first
            left[c, :, 2 * k * 128 : (2 * k + 1) * 128] = jnp.where(at, first, 0.0).astype(BF16)
            left[c, :, (2 * k + 1) * 128 : (2 * k + 2) * 128] = jnp.where(at, rest, 0.0).astype(BF16)
    for c in range(2):
        out_ref[pl.ds(c, 512, stride=2), :] = lax.dot_general(
            left[c], right[...], (((1,), (1,)), ((), ())), preferred_element_type=F32
        )


VM = pl.BlockSpec(memory_space=pltpu.VMEM)
SM = pl.BlockSpec(memory_space=pltpu.SMEM)


def shape(dims, dtype):
    return jax.ShapeDtypeStruct(dims, dtype)


def params():
    return pltpu.CompilerParams(vmem_limit_bytes=VMEM_LIMIT)


def cost(us):
    return pl.CostEstimate(flops=int(us * 1e9), bytes_accessed=int(us * 1e6), transcendentals=0)


def pick_call(me, owner, volume_rows, voxel_rows):
    own = owner.reshape(ROWS // 128, 128)
    return pl.pallas_call(
        pick_kernel,
        out_shape=(
            shape((ROWS // 128, 128), jnp.int32),
            shape((8, 128), jnp.int32),
            shape((8 * 12, 128), BF16),
        ),
        in_specs=[SM, VM, VM, VM, VM],
        out_specs=(VM, VM, VM),
        scratch_shapes=[pltpu.VMEM((ROWS // 128, 128), jnp.int32), pltpu.VMEM((96, 128), F32)],
        compiler_params=params(),
        name="pick_rows",
    )(me, own, own.T, volume_rows, voxel_rows)


def image_call(defocus, particle_rows):
    return pl.pallas_call(
        image_kernel,
        out_shape=(shape((PER * 512, KX), F32), shape((PER * KY, KX), F32)),
        in_specs=[SM, VM],
        out_specs=(VM, VM),
        scratch_shapes=[pltpu.VMEM((512, KX), F32)],
        compiler_params=params(),
        cost_estimate=cost(4),
        name="ctf_images",
    )(defocus, particle_rows)


def search_call(pos, noise, near, far, img, sq):
    tables = [jnp.asarray(t) for t in phase_constants()]
    return pl.pallas_call(
        search_kernel,
        out_shape=(shape((4 * HALF, KX), F32), shape((2 * HALF, KX), BF16)),
        in_specs=[SM, SM] + [VM] * 8,
        out_specs=(VM, VM),
        scratch_shapes=[
            pltpu.VMEM((4 * HALF, KX), F32),
            pltpu.VMEM((2 * KY, KX), F32),
            pltpu.VMEM((KY, PER * 2 * KX), BF16),
            pltpu.VMEM((PER * REFS, KX), F32),
            pltpu.VMEM((REFS * SHIFTS, 128), F32),
            pltpu.VMEM((REFS * SHIFTS, 128), BF16),
        ],
        compiler_params=params(),
        name="shift_search",
    )(pos, noise, near, far, img, sq, *tables)


def insert_call(mine, got):
    return pl.pallas_call(
        insert_kernel,
        out_shape=shape((1024, 128), F32),
        in_specs=[VM, VM],
        out_specs=VM,
        scratch_shapes=[
            pltpu.VMEM((96, 128), F32),
            pltpu.VMEM((2, 512, 2 * CAP * 128), BF16),
            pltpu.VMEM((128, 2 * CAP * 128), BF16),
        ],
        compiler_params=params(),
        name="insert_rows",
    )(mine, got)


def local(particles, defocus, inverse_noise, volume, slice_owner, slice_voxel):
    me = lax.axis_index(FINE).astype(jnp.int32).reshape(1)
    volume_rows = volume.reshape(2, 512, 128).transpose(1, 0, 2).reshape(1024, 128)
    pos, mine, compact = pick_call(me, slice_owner, volume_rows, slice_voxel.reshape(ROWS, KX))
    pos = pos.reshape(ROWS)
    line = lax.all_to_all(compact.reshape(8, CAP, 2, 128), ("zh", "zl"), 0, 0, tiled=True)
    spread = jnp.broadcast_to(line.reshape(1, 48, 2, 128), (32, 48, 2, 128))
    near = lax.all_to_all(spread, ("y", "x"), 0, 0, tiled=True).reshape(HALF, 2, 128)
    swap = [(0, 1), (1, 0)]
    far = lax.ppermute(near, "c", swap)
    img, sq = image_call(defocus, particles.reshape(PER * KY * 2, KX))
    sums, far_out = search_call(
        pos, inverse_noise, near.reshape(2 * HALF, 128), far.reshape(2 * HALF, 128), img, sq
    )
    received = lax.ppermute(far_out.reshape(HALF, 2, 128), "c", swap)
    pair = sums[: 2 * HALF].reshape(HALF, 2, 128) + received.astype(F32)
    plane = lax.all_to_all(pair.astype(BF16).reshape(32, 48, 2, 128), ("y", "x"), 0, 0, tiled=True)
    plane = jnp.sum(plane.astype(F32), axis=0).astype(BF16)
    last = lax.all_to_all(plane.reshape(8, CAP, 2, 128), ("zh", "zl"), 0, 0, tiled=True)
    out = insert_call(mine, last.reshape(96, 128))
    return out.reshape(512, 2, 128).transpose(1, 0, 2).reshape(2, 65536)


def solution(mesh):
    fine = Mesh(mesh.devices.reshape(4, 2, 8, 4, 2), FINE)
    in_specs = (P(FINE, None, None, None), P(FINE), P(FINE), P(None, FINE), P(), P())
    return jax.shard_map(local, mesh=fine, in_specs=in_specs, out_specs=P(None, FINE), check_vma=False)
```

time: 1490 us -> 123 us (0.08)
  the two profiles are of different devices: /device:TPU:1 before, /device:TPU:2 now
where the time goes in v1:
time: 123 us; the launch traced here: 122 us
  blocking collectives  87.4 us (71%)
  Pallas kernels  22.9 us (19%)
  starting transfers between devices  3.95 us (3%)
  local copies, waits for them, and re-layouts  3.52 us (3%)
  waiting for transfers between devices  2.83 us (2%)
  other arithmetic  1.53 us (1%)
    all_to_all x1, blocking collectives, local(): lax.all_to_all(spread, ('y', 'x'), 0, 0, tiled=True).reshape(HALF, 2, 128)  31.1 us
    all_to_all x1, blocking collectives, local(): lax.all_to_all(pair.astype(BF16).reshape(32, 48, 2, 128), ('y', 'x'), 0,...  28.1 us
    all_to_all x1, blocking collectives, local(): lax.all_to_all(compact.reshape(8, CAP, 2, 128), ('zh', 'zl'), 0, 0, tiled...  17.9 us
    pallas_call x1, Pallas kernels, search_call(): pl.pallas_call(search_kernel, out_shape=(shape((4 * HALF, KX), F32), shap...  17.9 us
    all_to_all x1, blocking collectives, local(): lax.all_to_all(plane.reshape(8, CAP, 2, 128), ('zh', 'zl'), 0, 0, tiled=T...  10.3 us
  transfers between devices with their start and end apart: 2, of which 2 were waited for; matrix products, arithmetic and copies ran while one was open for 0% of the time, Pallas kernels for 1%

profile of v1, /device:TPU:2, one launch (start us, length us, event | category | flops | bytes accessed | tf_op | source)
XLA Modules:
  0.0 122.3 jit_solution(11645602577475705297)
XLA Ops:
  0.0 0.7 reshape.54.own_ref
  0.7 0.1 copy.14
  0.8 0.0 copy-start
  0.8 1.2 copy-done
  2.0 0.0 copy-start.3
  2.0 0.9 copy-done.3
  3.0 0.0 copy-start.7
  3.0 0.0 copy-start.8
  3.0 1.8 %pick_rows.1 = (s32[16,128]{1,0:T(8,128)S(1)}, s32[8,128]{1,0:T(8,128)S(1)}, bf16[96,128]{1,0:T(8,128)(2,1)S(1)}) custom-call(s32[1]{0:T(128)} %bitcast.me_ref, s32[16,128]{1,0:T(8,128)S(1)} %reshape.54.own_ref, s32[128,16]{1,0:T(8,128)S(1)} %bitcast.30, bf16[1024,128]{1,0:T(8,128)(2,1)S(1)} %bitcast.29, s32[2048,128]{1,0:T(8,128)S(1)} %bitcast.27), custom_call_target="tpu_custom_call" | custom-call | tf_op jit(solution)/shard_map/pick_rows/pallas_call | solution.py:257
  4.8 17.9 %all_to_all.20 = bf16[8,6,2,128]{3,2,1,0:T(2,128)(2,1)S(1)} all-to-all(bf16[8,6,2,128]{3,2,1,0:T(2,128)(2,1)S(1)} %bitcast.32), channel_id=1, replica_groups=mesh['zh'=4,'c'=2,'y'=8,'x'=4,'zl'=2] {'zh','zl'}, dimensions={0} | all-to-all | bytes 49152 | tf_op jit(solution)/shard_map/all_to_all | solution.py:326
  22.7 0.4 broadcast_in_dim.8
  23.1 31.1 %all_to_all.21 = bf16[32,48,2,128]{3,2,1,0:T(2,128)(2,1)S(1)} all-to-all(bf16[32,48,2,128]{3,2,1,0:T(2,128)(2,1)S(1)} %broadcast_in_dim.8), channel_id=1, replica_groups=mesh['zh'=4,'c'=2,'y'=8,'x'=4,'zl'=2] {'y','x'}, dimensions={0} | all-to-all | bytes 1572864 | tf_op jit(solution)/shard_map/all_to_all | solution.py:328
  54.2 1.9 %collective-permute-start = (bf16[1536,2,128]{2,1,0:T(2,128)(2,1)S(1)}, bf16[1536,2,128]{2,1,0:T(2,128)(2,1)S(1)}, u32[]{:S(2)}, u32[]{:S(2)}) collective-permute-start(bf16[1536,2,128]{2,1,0:T(2,128)(2,1)S(1)} %bitcast.25), channel_id=1, source_target_pairs={{0,64},{64,0},{1,65},{65,1},{2,66},{66,2},{3,67},{67,3},{4,68},{68... | collective-permute-start | bytes 2359304 | tf_op jit(solution)/shard_map/ppermute | solution.py:330
  56.1 0.0 copy-done.7
  56.1 0.0 copy-done.8
  56.1 0.0 copy-start.1
  56.2 0.0 copy-start.2
  56.2 0.0 copy-start.4
  56.2 0.0 copy-start.5
  56.2 0.0 copy-start.6
  56.2 1.4 %ctf_images.1 = (f32[2048,128]{1,0:T(8,128)S(1)}, f32[1024,128]{1,0:T(8,128)S(1)}) custom-call(f32[4]{0:T(128)S(1)} %copy-done.8, bf16[2048,128]{1,0:T(8,128)(2,1)S(1)} %bitcast.35), custom_call_target="tpu_custom_call" | custom-call | flops 4000000000 | bytes 4000000 | tf_op jit(solution)/shard_map/ctf_images/pallas_call | solution.py:273
  57.6 0.8 collective-permute-done
  58.4 0.0 copy-done.1
  58.4 0.0 copy-done.2
  58.4 0.0 copy-done.4
  58.4 0.0 copy-done.5
  58.4 0.0 copy-done.6
  58.4 17.9 %shift_search.1 = (f32[6144,128]{1,0:T(8,128)S(1)}, bf16[3072,128]{1,0:T(8,128)(2,1)S(1)}) custom-call(s32[2048]{0:T(1024)S(1)} %bitcast.33, f32[4]{0:T(128)S(1)} %copy-done.6, bf16[3072,128]{1,0:T(8,128)(2,1)S(1)} %bitcast.26, bf16[3072,128]{1,0:T(8,128)(2,1)S(1)} %bitcast.28, f32[2048,128]{1,0:T(8,128)S(1)} %get-tuple-element.15.img_ref, ...), custom_call_target="tpu_custom_call" | custom-call | tf_op jit(solution)/shard_map/shift_search/pallas_call | solution.py:287
  76.3 2.0 %collective-permute-start.1 = (bf16[1536,2,128]{2,1,0:T(2,128)(2,1)S(1)}, bf16[1536,2,128]{2,1,0:T(2,128)(2,1)S(1)}, u32[]{:S(2)}, u32[]{:S(2)}) collective-permute-start(bf16[1536,2,128]{2,1,0:T(2,128)(2,1)S(1)} %bitcast.34), channel_id=1, source_target_pairs={{0,64},{64,0},{1,65},{65,1},{2,66},{66,2},{3,67},{67,3},{4,68},{68... | collective-permute-start | bytes 2359304 | tf_op jit(solution)/shard_map/ppermute | solution.py:335
  78.4 0.1 slice.3
  78.5 2.0 %collective-permute-done.1 = bf16[1536,2,128]{2,1,0:T(2,128)(2,1)S(1)} collective-permute-done((bf16[1536,2,128]{2,1,0:T(2,128)(2,1)S(1)}, bf16[1536,2,128]{2,1,0:T(2,128)(2,1)S(1)}, u32[]{:S(2)}, u32[]{:S(2)}) %collective-permute-start.1) | collective-permute-done | bytes 786464 | tf_op jit(solution)/shard_map/ppermute | solution.py:335
  80.5 0.8 add_convert_fusion
  81.3 28.1 %all_to_all.22 = bf16[32,48,2,128]{3,2,1,0:T(2,128)(2,1)S(1)} all-to-all(bf16[32,48,2,128]{3,2,1,0:T(2,128)(2,1)S(1)} %bitcast.37), channel_id=1, replica_groups=mesh['zh'=4,'c'=2,'y'=8,'x'=4,'zl'=2] {'y','x'}, dimensions={0} | all-to-all | bytes 1572864 | tf_op jit(solution)/shard_map/all_to_all | solution.py:337
  109.5 0.7 reduce_sum.12
  110.1 10.3 %all_to_all.23 = bf16[8,6,2,128]{3,2,1,0:T(2,128)(2,1)S(1)} all-to-all(bf16[8,6,2,128]{3,2,1,0:T(2,128)(2,1)S(1)} %bitcast.38), channel_id=1, replica_groups=mesh['zh'=4,'c'=2,'y'=8,'x'=4,'zl'=2] {'zh','zl'}, dimensions={0} | all-to-all | bytes 49152 | tf_op jit(solution)/shard_map/all_to_all | solution.py:339
  120.4 1.8 %insert_rows.1 = f32[1024,128]{1,0:T(8,128)} custom-call(s32[8,128]{1,0:T(8,128)S(1)} %get-tuple-element.12.mine_ref, bf16[96,128]{1,0:T(8,128)(2,1)S(1)} %bitcast.31), custom_call_target="tpu_custom_call" | custom-call | tf_op jit(solution)/shard_map/insert_rows/pallas_call | solution.py:306
Async XLA Ops:
  0.8 1.2 %copy-start = (s32[8,256,128]{2,1,0:T(8,128)S(1)}, s32[8,256,128]{2,1,0:T(8,128)}, u32[]{:S(2)}) copy-start(s32[8,256,128]{2,1,0:T(8,128)} %param.15) | copy-start | bytes 3145732
  2.0 0.9 copy-start.3
  3.0 53.1 %copy-start.7 = (bf16[4,256,2,128]{3,2,1,0:T(2,128)(2,1)S(1)}, bf16[4,256,2,128]{3,2,1,0:T(2,128)(2,1)}, u32[]{:S(2)}) copy-start(bf16[4,256,2,128]{3,2,1,0:T(2,128)(2,1)} %param.10) | copy-start | bytes 1572868
  3.0 53.1 %copy-start.8 = (f32[4]{0:T(128)S(1)}, f32[4]{0:T(128)}, u32[]{:S(2)}) copy-start(f32[4]{0:T(128)} %defocus_ref.1) | copy-start | bytes 52
  54.2 4.2 %collective-permute-start = (bf16[1536,2,128]{2,1,0:T(2,128)(2,1)S(1)}, bf16[1536,2,128]{2,1,0:T(2,128)(2,1)S(1)}, u32[]{:S(2)}, u32[]{:S(2)}) collective-permute-start(bf16[1536,2,128]{2,1,0:T(2,128)(2,1)S(1)} %bitcast.25), channel_id=1, source_target_pairs={{0,64},{64,0},{1,65},{65,1},{2,66},{66,2},{3,67},{67,3},{4,68},{68... | collective-permute-start | bytes 2359304 | tf_op jit(solution)/shard_map/ppermute | solution.py:330
  56.1 2.2 %copy-start.1 = (bf16[256,1024]{1,0:T(8,128)(2,1)S(1)}, bf16[256,1024]{1,0:T(8,128)(2,1)}, u32[]{:S(2)}) copy-start(bf16[256,1024]{1,0:T(8,128)(2,1)} %constant.39.clone.bwd_ref) | copy-start | bytes 1572868
  56.2 2.2 %copy-start.2 = (bf16[1024,256]{1,0:T(8,128)(2,1)S(1)}, bf16[1024,256]{1,0:T(8,128)(2,1)}, u32[]{:S(2)}) copy-start(bf16[1024,256]{1,0:T(8,128)(2,1)} %constant.38.clone.fwd_ref) | copy-start | bytes 1572868
  56.2 2.2 %copy-start.4 = (bf16[512,32]{1,0:T(8,128)(2,1)S(1)}, bf16[512,32]{1,0:T(8,128)(2,1)}, u32[]{:S(2)}) copy-start(bf16[512,32]{1,0:T(8,128)(2,1)} %constant.41.clone.back_ref) | copy-start | bytes 98308
  56.2 2.2 %copy-start.5 = (bf16[64,256]{1,0:T(8,128)(2,1)S(1)}, bf16[64,256]{1,0:T(8,128)(2,1)}, u32[]{:S(2)}) copy-start(bf16[64,256]{1,0:T(8,128)(2,1)} %constant.40.clone.corr_ref) | copy-start | bytes 98308
  56.2 2.2 %copy-start.6 = (f32[4]{0:T(128)S(1)}, f32[4]{0:T(128)}, u32[]{:S(2)}) copy-start(f32[4]{0:T(128)} %noise_ref.1) | copy-start | bytes 52
  76.3 4.2 %collective-permute-start.1 = (bf16[1536,2,128]{2,1,0:T(2,128)(2,1)S(1)}, bf16[1536,2,128]{2,1,0:T(2,128)(2,1)S(1)}, u32[]{:S(2)}, u32[]{:S(2)}) collective-permute-start(bf16[1536,2,128]{2,1,0:T(2,128)(2,1)S(1)} %bitcast.34), channel_id=1, source_target_pairs={{0,64},{64,0},{1,65},{65,1},{2,66},{66,2},{3,67},{67,3},{4,68},{68... | collective-permute-start | bytes 2359304 | tf_op jit(solution)/shard_map/ppermute | solution.py:335

commit v2 on v1

--- a/solution.py
+++ b/solution.py
@@ -48,39 +48,53 @@
     return lax.broadcasted_iota(jnp.int32, shape, dim)
 
 
-def pick_kernel(me_ref, own_ref, own_t_ref, vol_ref, vox_ref, pos_ref, mine_ref, out_ref, slot, stage):
+def pick_kernel(me_ref, own_ref, vol_hbm, vox_hbm, pos_ref, mine_ref, out_ref, slot, stage, table, near_rows, sems):
+    load = pltpu.make_async_copy(vol_hbm, table, sems.at[CAP])
+    load.start()
     me = me_ref[0]
-    blocks = ROWS // 128
-    cols = [jnp.broadcast_to(own_t_ref[:, c : c + 1], (128, 128)) for c in range(blocks)]
+    own = own_ref[...]
+    turned = own.astype(F32).T
+    cols, here = [], []
+    for b in range(ROWS // 128):
+        r, h = b // 2, b % 2
+        cols.append(jnp.broadcast_to(turned[h * 128 : (h + 1) * 128, r : r + 1], (128, 128)))
+        here.append(jnp.broadcast_to(own[r : r + 1, h * 128 : (h + 1) * 128].astype(F32), (128, 128)))
     earlier = iota((128, 128), 0) < iota((128, 128), 1)
-    for b in range(blocks):
-        here = jnp.broadcast_to(own_ref[b : b + 1, :], (128, 128))
-        hits = ((cols[b] == here) & earlier).astype(F32)
+    for b in range(ROWS // 128):
+        r, h = b // 2, b % 2
+        hits = ((cols[b] == here[b]) & earlier).astype(F32)
         for c in range(b):
-            hits = hits + (cols[c] == here).astype(F32)
-        slot[b : b + 1, :] = jnp.sum(hits, axis=0, keepdims=True).astype(jnp.int32)
-    own = own_ref[...]
+            hits = hits + (cols[c] == here[b]).astype(F32)
+        slot[r : r + 1, h * 128 : (h + 1) * 128] = jnp.sum(hits, axis=0, keepdims=True).astype(jnp.int32)
     slots = slot[...]
-    g1 = lax.shift_right_logical(own, 7) * 2 + (own & 1)
-    g2 = (lax.shift_right_logical(own, 3) & 7) * 4 + (lax.shift_right_logical(own, 1) & 3)
+    row_id = iota((REFS, KY), 0) * KY + iota((REFS, KY), 1)
+    is_me = own == me
+    found, loads = [], []
+    for k in range(CAP):
+        row = jnp.max(jnp.where(is_me & (slots == k), row_id, -1))
+        start = pl.multiple_of(jnp.maximum(row, 0) // 8 * 8, 8)
+        found.append(row)
+        loads.append(pltpu.make_async_copy(vox_hbm.at[pl.ds(start, 8), :], near_rows.at[k], sems.at[k]))
+        loads[k].start()
+    z = lax.shift_right_logical(own, 7) * 2 + (own & 1)
+    y = lax.shift_right_logical(own, 3) & 7
+    x = lax.shift_right_logical(own, 1) & 3
     across = ((lax.shift_right_logical(own, 6) ^ lax.shift_right_logical(me, 6)) & 1) * HALF
-    pos_ref[...] = across + g2 * 48 + g1 * CAP + jnp.minimum(slots, CAP - 1)
-    row_id = iota((blocks, 128), 0) * 128 + iota((blocks, 128), 1)
-    is_me = own == me
-    table = vol_ref[...]
+    pos_ref[...] = 2 * (across + x * (64 * CAP) + (z * 8 + y) * CAP + jnp.minimum(slots, CAP - 1))
     parity = (iota((8, 128), 0) & 1) == 0
     row_pair = lax.shift_right_logical(iota((1024, 128), 0), 1)
     lo_iota = iota((128, 128), 0)
+    sub = iota((8, 128), 0)
     mine_ref[...] = jnp.full((8, 128), -1, jnp.int32)
+    load.wait()
     for k in range(CAP):
-        hit = is_me & (slots == k)
-        row = jnp.max(jnp.where(hit, row_id, -1))
-        vox = vox_ref[pl.ds(jnp.maximum(row, 0), 1), :]
-        vox = jnp.where(row >= 0, vox, -1)
+        loads[k].wait()
+        vox = jnp.max(jnp.where(sub == (jnp.maximum(found[k], 0) & 7), near_rows[k], -1), axis=0, keepdims=True)
+        vox = jnp.where(found[k] >= 0, vox, -1)
         mine_ref[k : k + 1, :] = vox
         hi = lax.shift_right_arithmetic(vox, 7)
         onehot = (lo_iota == (vox & 127)).astype(F32).astype(BF16)
-        wide = jnp.dot(table, onehot, preferred_element_type=F32)
+        wide = jnp.dot(table[...], onehot, preferred_element_type=F32)
         kept = jnp.where(row_pair == hi, wide, 0.0)
         kept = jnp.sum(kept.reshape(128, 8, 128), axis=0)
         re = jnp.sum(jnp.where(parity, kept, 0.0), axis=0, keepdims=True)
@@ -88,7 +102,9 @@
         for copy in range(8):
             stage[copy * 12 + 2 * k : copy * 12 + 2 * k + 1, :] = re
             stage[copy * 12 + 2 * k + 1 : copy * 12 + 2 * k + 2, :] = im
-    out_ref[...] = stage[...].astype(BF16)
+    block = stage[...].astype(BF16)
+    for copy in range(8):
+        out_ref[copy * 96 : (copy + 1) * 96, :] = block
 
 
 def image_kernel(defocus_ref, part_ref, img_ref, sq_ref, wide):
@@ -121,28 +137,33 @@
 
 
 def search_kernel(pos_ref, noise_ref, near_ref, far_ref, img_ref, sq_ref, fwd_ref, bwd_ref, corr_ref, back_ref,
-                  sum_ref, far_out_ref, slots, rows, q, power, corr, weight):
+                  sum_ref, far_out_ref, slots, rows_a, rows_b, q_a, q_b, power, corr, weight):
     slots[0 : 2 * HALF, :] = near_ref[...].astype(F32)
     slots[2 * HALF : 4 * HALF, :] = far_ref[...].astype(F32)
-    sum_ref[...] = jnp.zeros_like(sum_ref)
-
-    def forward(r, carry):
-        def fetch(g, c):
-            for u in range(32):
-                y = g * 32 + u
-                at = pl.multiple_of(2 * pos_ref[r * KY + y], 2)
-                rows[pl.ds(pl.multiple_of(2 * y, 2), 2), :] = slots[pl.ds(at, 2), :]
-            return c
-
-        lax.fori_loop(0, KY // 32, fetch, 0)
+
+    def fetch(r, rows, k):
+        for y in range(k * CH, (k + 1) * CH):
+            at = pl.multiple_of(pos_ref[r, y], 2)
+            rows[2 * y : 2 * y + 2, :] = slots[pl.ds(at, 2), :]
+
+    def put(r, rows, k):
+        for y in range(k * CH, (k + 1) * CH):
+            at = pl.multiple_of(pos_ref[r, y], 2)
+            sum_ref[pl.ds(at, 2), :] = rows[2 * y : 2 * y + 2, :]
+
+    def images(p, k):
+        at = p * 512 + k * CH
+        return img_ref[at : at + CH, :], img_ref[at + KY : at + KY + CH, :]
+
+    def score_ref(r, rows, q, ahead, ahead_rows):
         sums = [jnp.zeros((8, KX), F32) for _ in range(PER)]
         for k in range(KY // CH):
+            fetch(ahead, ahead_rows, k)
             re = rows[pl.ds(2 * CH * k, CH, stride=2), :]
             im = rows[pl.ds(2 * CH * k + 1, CH, stride=2), :]
             mag = re * re + im * im
             for p in range(PER):
-                a_re = img_ref[p * 512 + k * CH : p * 512 + (k + 1) * CH, :]
-                a_im = img_ref[p * 512 + KY + k * CH : p * 512 + KY + (k + 1) * CH, :]
+                a_re, a_im = images(p, k)
                 q[k * CH : (k + 1) * CH, p * 256 : p * 256 + 128] = (re * a_re + im * a_im).astype(BF16)
                 q[k * CH : (k + 1) * CH, p * 256 + 128 : (p + 1) * 256] = (re * a_im - im * a_re).astype(BF16)
                 part = sq_ref[p * KY + k * CH : p * KY + (k + 1) * CH, :] * mag
@@ -152,9 +173,16 @@
         row_phase = jnp.dot(q[...], fwd_ref[...], preferred_element_type=F32).astype(BF16)
         both = jnp.dot(corr_ref[...], row_phase, preferred_element_type=F32)
         corr[pl.ds(pl.multiple_of(r * SHIFTS, SHIFTS), SHIFTS), :] = both[:SHIFTS, :128] - both[SHIFTS:, 128:]
+
+    def forward(t, carry):
+        r = 2 * t
+        score_ref(r, rows_a, q_a, r + 1, rows_b)
+        score_ref(r + 1, rows_b, q_b, jnp.minimum(r + 2, REFS - 1), rows_a)
         return carry
 
-    lax.fori_loop(0, REFS, forward, 0)
+    for k in range(KY // CH):
+        fetch(0, rows_a, k)
+    lax.fori_loop(0, REFS // 2, forward, 0)
 
     group = lax.shift_right_logical(iota((1, 128), 1), 5)
     noise = jnp.zeros((1, 128), F32)
@@ -175,17 +203,18 @@
     for p in range(PER):
         norm = jnp.where(group == p, jnp.sum(jnp.where(group == p, lane_sum, 0.0), axis=1, keepdims=True), norm)
     weight[...] = (expo * (1.0 / norm)).astype(BF16)
-
-    def backward(r, carry):
+    sum_ref[...] = jnp.zeros_like(sum_ref)
+
+    def insert_ref(r, rows, behind, behind_rows):
         w = weight[pl.ds(pl.multiple_of(r * SHIFTS, SHIFTS), SHIFTS), :]
         col = jnp.dot(back_ref[...], w, preferred_element_type=F32).astype(BF16)
         col = jnp.concatenate([col[:KY], col[KY:]], axis=1)
         for k in range(KY // CH):
+            put(behind, behind_rows, k)
             ss = jnp.dot(col[k * CH : (k + 1) * CH], bwd_ref[...], preferred_element_type=F32).astype(BF16).astype(F32)
             t_re = t_im = None
             for p in range(PER):
-                a_re = img_ref[p * 512 + k * CH : p * 512 + (k + 1) * CH, :]
-                a_im = img_ref[p * 512 + KY + k * CH : p * 512 + KY + (k + 1) * CH, :]
+                a_re, a_im = images(p, k)
                 s_re = ss[:, p * 256 : p * 256 + 128]
                 s_im = ss[:, p * 256 + 128 : (p + 1) * 256]
                 u_re = a_re * s_re - a_im * s_im
@@ -195,23 +224,21 @@
             rows[pl.ds(2 * CH * k, CH, stride=2), :] = t_re
             rows[pl.ds(2 * CH * k + 1, CH, stride=2), :] = t_im
 
-        def put(g, c):
-            for u in range(32):
-                y = g * 32 + u
-                at = pl.multiple_of(2 * pos_ref[r * KY + y], 2)
-                sum_ref[pl.ds(at, 2), :] = rows[pl.ds(pl.multiple_of(2 * y, 2), 2), :]
-            return c
-
-        lax.fori_loop(0, KY // 32, put, 0)
+    def backward(t, carry):
+        r = 2 * t
+        insert_ref(r, rows_a, (r + REFS - 1) % REFS, rows_b)
+        insert_ref(r + 1, rows_b, r, rows_a)
         return carry
 
-    lax.fori_loop(0, REFS, backward, 0)
+    lax.fori_loop(0, REFS // 2, backward, 0)
+    for k in range(KY // CH):
+        put(REFS - 1, rows_b, k)
     far_out_ref[...] = sum_ref[2 * HALF : 4 * HALF, :].astype(BF16)
 
 
 def insert_kernel(mine_ref, got_ref, out_ref, wide, left, right):
-    wide[...] = got_ref[...].astype(F32)
-    scale = 1.0 / math.sqrt(PARTICLES)
+    sums = jnp.sum(got_ref[...].astype(F32).reshape(32, 24, 128), axis=0)
+    wide[...] = sums * (1.0 / math.sqrt(PARTICLES))
     hi_iota = iota((512, 128), 0)
     lo_iota = iota((128, 128), 0)
     for k in range(CAP):
@@ -222,10 +249,7 @@
         right[:, (2 * k + 1) * 128 : (2 * k + 2) * 128] = onehot
         at = hi_iota == hi
         for c in range(2):
-            total = jnp.zeros((1, 128), F32)
-            for src in range(8):
-                total = total + wide[src * 12 + 2 * k + c : src * 12 + 2 * k + c + 1, :]
-            total = total * scale
+            total = wide[2 * k + c : 2 * k + c + 1, :] + wide[12 + 2 * k + c : 12 + 2 * k + c + 1, :]
             first = total.astype(BF16).astype(F32)
             rest = total - first
             left[c, :, 2 * k * 128 : (2 * k + 1) * 128] = jnp.where(at, first, 0.0).astype(BF16)
@@ -238,6 +262,7 @@
 
 VM = pl.BlockSpec(memory_space=pltpu.VMEM)
 SM = pl.BlockSpec(memory_space=pltpu.SMEM)
+ANY = pl.BlockSpec(memory_space=pl.ANY)
 
 
 def shape(dims, dtype):
@@ -253,20 +278,25 @@
 
 
 def pick_call(me, owner, volume_rows, voxel_rows):
-    own = owner.reshape(ROWS // 128, 128)
     return pl.pallas_call(
         pick_kernel,
         out_shape=(
-            shape((ROWS // 128, 128), jnp.int32),
+            shape((REFS, KY), jnp.int32),
             shape((8, 128), jnp.int32),
-            shape((8 * 12, 128), BF16),
+            shape((64 * 12, 128), BF16),
         ),
-        in_specs=[SM, VM, VM, VM, VM],
+        in_specs=[SM, VM, ANY, ANY],
         out_specs=(VM, VM, VM),
-        scratch_shapes=[pltpu.VMEM((ROWS // 128, 128), jnp.int32), pltpu.VMEM((96, 128), F32)],
-        compiler_params=params(),
+        scratch_shapes=[
+            pltpu.VMEM((REFS, KY), jnp.int32),
+            pltpu.VMEM((96, 128), F32),
+            pltpu.VMEM((1024, 128), BF16),
+            pltpu.VMEM((CAP, 8, 128), jnp.int32),
+            pltpu.SemaphoreType.DMA((CAP + 1,)),
+        ],
+        compiler_params=pltpu.CompilerParams(vmem_limit_bytes=60 * 1024 * 1024),
         name="pick_rows",
-    )(me, own, own.T, volume_rows, voxel_rows)
+    )(me, owner, volume_rows, voxel_rows)
 
 
 def image_call(defocus, particle_rows):
@@ -292,6 +322,8 @@
         scratch_shapes=[
             pltpu.VMEM((4 * HALF, KX), F32),
             pltpu.VMEM((2 * KY, KX), F32),
+            pltpu.VMEM((2 * KY, KX), F32),
+            pltpu.VMEM((KY, PER * 2 * KX), BF16),
             pltpu.VMEM((KY, PER * 2 * KX), BF16),
             pltpu.VMEM((PER * REFS, KX), F32),
             pltpu.VMEM((REFS * SHIFTS, 128), F32),
@@ -309,7 +341,7 @@
         in_specs=[VM, VM],
         out_specs=VM,
         scratch_shapes=[
-            pltpu.VMEM((96, 128), F32),
+            pltpu.VMEM((24, 128), F32),
             pltpu.VMEM((2, 512, 2 * CAP * 128), BF16),
             pltpu.VMEM((128, 2 * CAP * 128), BF16),
         ],
@@ -322,10 +354,9 @@
     me = lax.axis_index(FINE).astype(jnp.int32).reshape(1)
     volume_rows = volume.reshape(2, 512, 128).transpose(1, 0, 2).reshape(1024, 128)
     pos, mine, compact = pick_call(me, slice_owner, volume_rows, slice_voxel.reshape(ROWS, KX))
-    pos = pos.reshape(ROWS)
-    line = lax.all_to_all(compact.reshape(8, CAP, 2, 128), ("zh", "zl"), 0, 0, tiled=True)
-    spread = jnp.broadcast_to(line.reshape(1, 48, 2, 128), (32, 48, 2, 128))
-    near = lax.all_to_all(spread, ("y", "x"), 0, 0, tiled=True).reshape(HALF, 2, 128)
+    line = lax.all_to_all(compact.reshape(64, CAP, 2, 128), ("zh", "zl", "y"), 0, 0, tiled=True)
+    spread = jnp.broadcast_to(line.reshape(1, 384, 2, 128), (4, 384, 2, 128))
+    near = lax.all_to_all(spread, "x", 0, 0, tiled=True).reshape(HALF, 2, 128)
     swap = [(0, 1), (1, 0)]
     far = lax.ppermute(near, "c", swap)
     img, sq = image_call(defocus, particles.reshape(PER * KY * 2, KX))
@@ -334,10 +365,10 @@
     )
     received = lax.ppermute(far_out.reshape(HALF, 2, 128), "c", swap)
     pair = sums[: 2 * HALF].reshape(HALF, 2, 128) + received.astype(F32)
-    plane = lax.all_to_all(pair.astype(BF16).reshape(32, 48, 2, 128), ("y", "x"), 0, 0, tiled=True)
+    plane = lax.all_to_all(pair.astype(BF16).reshape(4, 384, 2, 128), "x", 0, 0, tiled=True)
     plane = jnp.sum(plane.astype(F32), axis=0).astype(BF16)
-    last = lax.all_to_all(plane.reshape(8, CAP, 2, 128), ("zh", "zl"), 0, 0, tiled=True)
-    out = insert_call(mine, last.reshape(96, 128))
+    last = lax.all_to_all(plane.reshape(64, CAP, 2, 128), ("zh", "zl", "y"), 0, 0, tiled=True)
+    out = insert_call(mine, last.reshape(768, 128))
     return out.reshape(512, 2, 128).transpose(1, 0, 2).reshape(2, 65536)
 
 

time: 123 us -> 109 us (0.89)
  the two profiles are of different devices: /device:TPU:2 before, /device:TPU:8 now
where the time goes in v2:
time: 109 us
  blocking collectives  78 us (72%)
  Pallas kernels  21.4 us (20%)
  starting transfers between devices  3.96 us (4%)
  waiting for transfers between devices  2.81 us (3%)
  other arithmetic  1.98 us (2%)
    all_to_all x1, blocking collectives, local(): lax.all_to_all(compact.reshape(64, CAP, 2, 128), ('zh', 'zl', 'y'), 0, 0,...  29.9 us
    all_to_all x1, blocking collectives, local(): lax.all_to_all(plane.reshape(64, CAP, 2, 128), ('zh', 'zl', 'y'), 0, 0, t...  18.4 us
    all_to_all x1, blocking collectives, local(): lax.all_to_all(pair.astype(BF16).reshape(4, 384, 2, 128), 'x', 0, 0, tile...  15.3 us
    all_to_all x1, blocking collectives, local(): near = lax.all_to_all(spread, 'x', 0, 0, tiled=True).reshape(HALF, 2, 128)  14.4 us
    pallas_call x1, Pallas kernels, search_call(): pl.pallas_call(search_kernel, out_shape=(shape((4 * HALF, KX), F32), shap...  12.9 us
    pallas_call x1, Pallas kernels, pick_call(): pl.pallas_call(pick_kernel, out_shape=(shape((REFS, KY), jnp.int32), shap...  5.24 us
  transfers between devices with their start and end apart: 2, of which 2 were waited for; matrix products, arithmetic and copies ran while one was open for 0% of the time, Pallas kernels for 1%

profile of v2, /device:TPU:8, one launch (start us, length us, event | category | flops | bytes accessed | tf_op | source)
XLA Modules:
  0.0 108.9 jit_solution(12886306852547267118)
XLA Ops:
  0.0 5.2 %pick_rows.1 = (s32[8,256]{1,0:T(8,128)}, s32[8,128]{1,0:T(8,128)}, bf16[768,128]{1,0:T(8,128)(2,1)}) custom-call(s32[1]{0:T(128)} %bitcast.me_ref, s32[8,256]{1,0:T(8,128)} %own_ref.1, bf16[1024,128]{1,0:T(8,128)(2,1)} %bitcast.34, s32[2048,128]{1,0:T(8,128)} %bitcast.31), custom_call_target="tpu_custom_call" | custom-call | tf_op jit(solution)/shard_map/pick_rows/pallas_call | solution.py:281
  5.3 0.0 copy-start.7
  5.3 0.0 copy-start.8
  5.3 29.9 %all_to_all.20 = bf16[64,6,2,128]{3,2,1,0:T(2,128)(2,1)S(1)} all-to-all(bf16[64,6,2,128]{3,2,1,0:T(2,128)(2,1)} %bitcast.35), channel_id=1, replica_groups=mesh['zh'=4,'c'=2,'y'=8,'x'=4,'zl'=2] {'zh','zl','y'}, dimensions={0} | all-to-all | bytes 393216 | tf_op jit(solution)/shard_map/all_to_all | solution.py:357
  35.2 0.4 broadcast_in_dim.8
  35.6 14.4 %all_to_all.21 = bf16[4,384,2,128]{3,2,1,0:T(2,128)(2,1)S(1)} all-to-all(bf16[4,384,2,128]{3,2,1,0:T(2,128)(2,1)S(1)} %broadcast_in_dim.8), channel_id=1, replica_groups=mesh['zh'=4,'c'=2,'y'=8,'x'=4,'zl'=2] {'x'}, dimensions={0} | all-to-all | bytes 1572864 | tf_op jit(solution)/shard_map/all_to_all | solution.py:359
  50.0 1.9 %collective-permute-start = (bf16[1536,2,128]{2,1,0:T(2,128)(2,1)S(1)}, bf16[1536,2,128]{2,1,0:T(2,128)(2,1)S(1)}, u32[]{:S(2)}, u32[]{:S(2)}) collective-permute-start(bf16[1536,2,128]{2,1,0:T(2,128)(2,1)S(1)} %bitcast.23), channel_id=1, source_target_pairs={{0,64},{64,0},{1,65},{65,1},{2,66},{66,2},{3,67},{67,3},{4,68},{68... | collective-permute-start | bytes 2359304 | tf_op jit(solution)/shard_map/ppermute | solution.py:361
  51.9 0.0 copy-done.7
  51.9 0.0 copy-done.8
  51.9 0.0 copy-start
  51.9 0.0 copy-start.1
  51.9 0.0 copy-start.2
  52.0 0.0 copy-start.3
  52.0 0.0 copy-start.4
  52.0 0.0 copy-start.6
  52.0 1.4 %ctf_images.1 = (f32[2048,128]{1,0:T(8,128)S(1)}, f32[1024,128]{1,0:T(8,128)S(1)}) custom-call(f32[4]{0:T(128)S(1)} %copy-done.8, bf16[2048,128]{1,0:T(8,128)(2,1)S(1)} %bitcast.28), custom_call_target="tpu_custom_call" | custom-call | flops 4000000000 | bytes 4000000 | tf_op jit(solution)/shard_map/ctf_images/pallas_call | solution.py:303
  53.4 0.8 collective-permute-done
  54.2 0.0 copy-done
  54.2 0.0 copy-done.1
  54.2 0.0 copy-done.2
  54.2 0.0 copy-done.3
  54.2 0.0 copy-done.4
  54.2 0.0 copy-done.6
  54.2 12.9 %shift_search.1 = (f32[6144,128]{1,0:T(8,128)S(1)}, bf16[3072,128]{1,0:T(8,128)(2,1)S(1)}) custom-call(s32[8,256]{1,0:T(8,128)S(1)} %copy-done.4, f32[4]{0:T(128)S(1)} %copy-done.6, bf16[3072,128]{1,0:T(8,128)(2,1)S(1)} %bitcast.24, bf16[3072,128]{1,0:T(8,128)(2,1)S(1)} %bitcast.25, f32[2048,128]{1,0:T(8,128)S(1)} %get-tuple-element.15.img_ref, ...), custom_call_target="tpu_custom_call" | custom-call | tf_op jit(solution)/shard_map/shift_search/pallas_call | solution.py:317
  67.1 2.0 %collective-permute-start.1 = (bf16[1536,2,128]{2,1,0:T(2,128)(2,1)S(1)}, bf16[1536,2,128]{2,1,0:T(2,128)(2,1)S(1)}, u32[]{:S(2)}, u32[]{:S(2)}) collective-permute-start(bf16[1536,2,128]{2,1,0:T(2,128)(2,1)S(1)} %bitcast.27), channel_id=1, source_target_pairs={{0,64},{64,0},{1,65},{65,1},{2,66},{66,2},{3,67},{67,3},{4,68},{68... | collective-permute-start | bytes 2359304 | tf_op jit(solution)/shard_map/ppermute | solution.py:366
  69.2 0.1 slice.3
  69.3 2.0 %collective-permute-done.1 = bf16[1536,2,128]{2,1,0:T(2,128)(2,1)S(1)} collective-permute-done((bf16[1536,2,128]{2,1,0:T(2,128)(2,1)S(1)}, bf16[1536,2,128]{2,1,0:T(2,128)(2,1)S(1)}, u32[]{:S(2)}, u32[]{:S(2)}) %collective-permute-start.1) | collective-permute-done | bytes 786464 | tf_op jit(solution)/shard_map/ppermute | solution.py:366
  71.3 0.8 add_convert_fusion
  72.2 0.0 copy-start.5
  72.2 15.3 %all_to_all.22 = bf16[4,384,2,128]{3,2,1,0:T(2,128)(2,1)S(1)} all-to-all(bf16[4,384,2,128]{3,2,1,0:T(2,128)(2,1)S(1)} %bitcast.30), channel_id=1, replica_groups=mesh['zh'=4,'c'=2,'y'=8,'x'=4,'zl'=2] {'x'}, dimensions={0} | all-to-all | bytes 1572864 | tf_op jit(solution)/shard_map/all_to_all | solution.py:368
  87.5 1.1 %reduce_sum.12 = bf16[384,2,128]{2,1,0:T(2,128)(2,1)S(1)} reduce(bf16[4,384,2,128]{3,2,1,0:T(2,128)(2,1)S(1)} %all_to_all.22, bf16[]{:T(256)} %constant.37.clone.1), dimensions={0}, to_apply=%region_0.0 | reduce | flops 294912 | bytes 983042 | tf_op jit(solution)/shard_map/reduce_sum | solution.py:369
  88.6 18.4 %all_to_all.23 = bf16[64,6,2,128]{3,2,1,0:T(2,128)(2,1)S(1)} all-to-all(bf16[64,6,2,128]{3,2,1,0:T(2,128)(2,1)S(1)} %bitcast.32), channel_id=1, replica_groups=mesh['zh'=4,'c'=2,'y'=8,'x'=4,'zl'=2] {'zh','zl','y'}, dimensions={0} | all-to-all | bytes 393216 | tf_op jit(solution)/shard_map/all_to_all | solution.py:370
  107.0 0.0 copy-done.5
  107.0 1.9 %insert_rows.1 = f32[1024,128]{1,0:T(8,128)} custom-call(s32[8,128]{1,0:T(8,128)S(1)} %copy-done.5, bf16[768,128]{1,0:T(8,128)(2,1)S(1)} %bitcast.26), custom_call_target="tpu_custom_call" | custom-call | tf_op jit(solution)/shard_map/insert_rows/pallas_call | solution.py:338
Async XLA Ops:
  5.3 46.7 %copy-start.7 = (bf16[4,256,2,128]{3,2,1,0:T(2,128)(2,1)S(1)}, bf16[4,256,2,128]{3,2,1,0:T(2,128)(2,1)}, u32[]{:S(2)}) copy-start(bf16[4,256,2,128]{3,2,1,0:T(2,128)(2,1)} %param.10) | copy-start | bytes 1572868
  5.3 46.6 %copy-start.8 = (f32[4]{0:T(128)S(1)}, f32[4]{0:T(128)}, u32[]{:S(2)}) copy-start(f32[4]{0:T(128)} %defocus_ref.1) | copy-start | bytes 52
  50.0 4.2 %collective-permute-start = (bf16[1536,2,128]{2,1,0:T(2,128)(2,1)S(1)}, bf16[1536,2,128]{2,1,0:T(2,128)(2,1)S(1)}, u32[]{:S(2)}, u32[]{:S(2)}) collective-permute-start(bf16[1536,2,128]{2,1,0:T(2,128)(2,1)S(1)} %bitcast.23), channel_id=1, source_target_pairs={{0,64},{64,0},{1,65},{65,1},{2,66},{66,2},{3,67},{67,3},{4,68},{68... | collective-permute-start | bytes 2359304 | tf_op jit(solution)/shard_map/ppermute | solution.py:361
  51.9 2.2 %copy-start = (bf16[256,1024]{1,0:T(8,128)(2,1)S(1)}, bf16[256,1024]{1,0:T(8,128)(2,1)}, u32[]{:S(2)}) copy-start(bf16[256,1024]{1,0:T(8,128)(2,1)} %constant.39.clone.bwd_ref) | copy-start | bytes 1572868
  51.9 2.2 %copy-start.1 = (bf16[1024,256]{1,0:T(8,128)(2,1)S(1)}, bf16[1024,256]{1,0:T(8,128)(2,1)}, u32[]{:S(2)}) copy-start(bf16[1024,256]{1,0:T(8,128)(2,1)} %constant.38.clone.fwd_ref) | copy-start | bytes 1572868
  51.9 2.2 %copy-start.2 = (bf16[512,32]{1,0:T(8,128)(2,1)S(1)}, bf16[512,32]{1,0:T(8,128)(2,1)}, u32[]{:S(2)}) copy-start(bf16[512,32]{1,0:T(8,128)(2,1)} %constant.41.clone.back_ref) | copy-start | bytes 98308
  52.0 2.2 %copy-start.3 = (bf16[64,256]{1,0:T(8,128)(2,1)S(1)}, bf16[64,256]{1,0:T(8,128)(2,1)}, u32[]{:S(2)}) copy-start(bf16[64,256]{1,0:T(8,128)(2,1)} %constant.40.clone.corr_ref) | copy-start | bytes 98308
  52.0 2.2 %copy-start.4 = (s32[8,256]{1,0:T(8,128)S(1)}, s32[8,256]{1,0:T(8,128)}, u32[]{:S(2)}) copy-start(s32[8,256]{1,0:T(8,128)} %get-tuple-element.13.pos_ref) | copy-start | bytes 24580
  52.0 2.2 %copy-start.6 = (f32[4]{0:T(128)S(1)}, f32[4]{0:T(128)}, u32[]{:S(2)}) copy-start(f32[4]{0:T(128)} %noise_ref.1) | copy-start | bytes 52
  67.1 4.2 %collective-permute-start.1 = (bf16[1536,2,128]{2,1,0:T(2,128)(2,1)S(1)}, bf16[1536,2,128]{2,1,0:T(2,128)(2,1)S(1)}, u32[]{:S(2)}, u32[]{:S(2)}) collective-permute-start(bf16[1536,2,128]{2,1,0:T(2,128)(2,1)S(1)} %bitcast.27), channel_id=1, source_target_pairs={{0,64},{64,0},{1,65},{65,1},{2,66},{66,2},{3,67},{67,3},{4,68},{68... | collective-permute-start | bytes 2359304 | tf_op jit(solution)/shard_map/ppermute | solution.py:366
  72.2 34.8 %copy-start.5 = (s32[8,128]{1,0:T(8,128)S(1)}, s32[8,128]{1,0:T(8,128)}, u32[]{:S(2)}) copy-start(s32[8,128]{1,0:T(8,128)} %get-tuple-element.12.mine_ref) | copy-start | bytes 12292

commit v3 on v2

--- a/solution.py
+++ b/solution.py
@@ -48,11 +48,16 @@
     return lax.broadcasted_iota(jnp.int32, shape, dim)
 
 
-def pick_kernel(me_ref, own_ref, vol_hbm, vox_hbm, pos_ref, mine_ref, out_ref, slot, stage, table, near_rows, sems):
-    load = pltpu.make_async_copy(vol_hbm, table, sems.at[CAP])
-    load.start()
+def pick_kernel(me_ref, own_hbm, vol_hbm, vox_hbm, pos_ref, mine_ref, out_ref, owners, slot, stage, table, voxels, sems):
+    load_own = pltpu.make_async_copy(own_hbm, owners, sems.at[0])
+    load_vox = pltpu.make_async_copy(vox_hbm, voxels, sems.at[1])
+    load_vol = pltpu.make_async_copy(vol_hbm, table, sems.at[2])
+    load_own.start()
+    load_vox.start()
+    load_vol.start()
     me = me_ref[0]
-    own = own_ref[...]
+    load_own.wait()
+    own = owners[...]
     turned = own.astype(F32).T
     cols, here = [], []
     for b in range(ROWS // 128):
@@ -69,13 +74,7 @@
     slots = slot[...]
     row_id = iota((REFS, KY), 0) * KY + iota((REFS, KY), 1)
     is_me = own == me
-    found, loads = [], []
-    for k in range(CAP):
-        row = jnp.max(jnp.where(is_me & (slots == k), row_id, -1))
-        start = pl.multiple_of(jnp.maximum(row, 0) // 8 * 8, 8)
-        found.append(row)
-        loads.append(pltpu.make_async_copy(vox_hbm.at[pl.ds(start, 8), :], near_rows.at[k], sems.at[k]))
-        loads[k].start()
+    found = [jnp.max(jnp.where(is_me & (slots == k), row_id, -1)) for k in range(CAP)]
     z = lax.shift_right_logical(own, 7) * 2 + (own & 1)
     y = lax.shift_right_logical(own, 3) & 7
     x = lax.shift_right_logical(own, 1) & 3
@@ -84,12 +83,11 @@
     parity = (iota((8, 128), 0) & 1) == 0
     row_pair = lax.shift_right_logical(iota((1024, 128), 0), 1)
     lo_iota = iota((128, 128), 0)
-    sub = iota((8, 128), 0)
     mine_ref[...] = jnp.full((8, 128), -1, jnp.int32)
-    load.wait()
+    load_vox.wait()
+    load_vol.wait()
     for k in range(CAP):
-        loads[k].wait()
-        vox = jnp.max(jnp.where(sub == (jnp.maximum(found[k], 0) & 7), near_rows[k], -1), axis=0, keepdims=True)
+        vox = voxels[pl.ds(jnp.maximum(found[k], 0), 1), :]
         vox = jnp.where(found[k] >= 0, vox, -1)
         mine_ref[k : k + 1, :] = vox
         hi = lax.shift_right_arithmetic(vox, 7)
@@ -209,9 +207,10 @@
         w = weight[pl.ds(pl.multiple_of(r * SHIFTS, SHIFTS), SHIFTS), :]
         col = jnp.dot(back_ref[...], w, preferred_element_type=F32).astype(BF16)
         col = jnp.concatenate([col[:KY], col[KY:]], axis=1)
+        shifted = jnp.dot(col, bwd_ref[...], preferred_element_type=F32).astype(BF16)
         for k in range(KY // CH):
             put(behind, behind_rows, k)
-            ss = jnp.dot(col[k * CH : (k + 1) * CH], bwd_ref[...], preferred_element_type=F32).astype(BF16).astype(F32)
+            ss = shifted[k * CH : (k + 1) * CH].astype(F32)
             t_re = t_im = None
             for p in range(PER):
                 a_re, a_im = images(p, k)
@@ -260,6 +259,17 @@
         )
 
 
+def pair_kernel(sums_ref, got_ref, out_ref):
+    out_ref[...] = (sums_ref[0 : 2 * HALF, :] + got_ref[...].astype(F32)).astype(BF16)
+
+
+def line_kernel(got_ref, out_ref):
+    total = got_ref[0:768, :].astype(F32)
+    for k in range(1, 4):
+        total = total + got_ref[k * 768 : (k + 1) * 768, :].astype(F32)
+    out_ref[...] = total.astype(BF16)
+
+
 VM = pl.BlockSpec(memory_space=pltpu.VMEM)
 SM = pl.BlockSpec(memory_space=pltpu.SMEM)
 ANY = pl.BlockSpec(memory_space=pl.ANY)
@@ -285,14 +295,15 @@
             shape((8, 128), jnp.int32),
             shape((64 * 12, 128), BF16),
         ),
-        in_specs=[SM, VM, ANY, ANY],
+        in_specs=[SM, ANY, ANY, ANY],
         out_specs=(VM, VM, VM),
         scratch_shapes=[
             pltpu.VMEM((REFS, KY), jnp.int32),
+            pltpu.VMEM((REFS, KY), jnp.int32),
             pltpu.VMEM((96, 128), F32),
             pltpu.VMEM((1024, 128), BF16),
-            pltpu.VMEM((CAP, 8, 128), jnp.int32),
-            pltpu.SemaphoreType.DMA((CAP + 1,)),
+            pltpu.VMEM((ROWS, KX), jnp.int32),
+            pltpu.SemaphoreType.DMA((3,)),
         ],
         compiler_params=pltpu.CompilerParams(vmem_limit_bytes=60 * 1024 * 1024),
         name="pick_rows",
@@ -334,6 +345,17 @@
     )(pos, noise, near, far, img, sq, *tables)
 
 
+def small_call(kernel, name, rows, *args):
+    return pl.pallas_call(
+        kernel,
+        out_shape=shape((rows, 128), BF16),
+        in_specs=[VM] * len(args),
+        out_specs=VM,
+        compiler_params=params(),
+        name=name,
+    )(*args)
+
+
 def insert_call(mine, got):
     return pl.pallas_call(
         insert_kernel,
@@ -364,9 +386,9 @@
         pos, inverse_noise, near.reshape(2 * HALF, 128), far.reshape(2 * HALF, 128), img, sq
     )
     received = lax.ppermute(far_out.reshape(HALF, 2, 128), "c", swap)
-    pair = sums[: 2 * HALF].reshape(HALF, 2, 128) + received.astype(F32)
-    plane = lax.all_to_all(pair.astype(BF16).reshape(4, 384, 2, 128), "x", 0, 0, tiled=True)
-    plane = jnp.sum(plane.astype(F32), axis=0).astype(BF16)
+    pair = small_call(pair_kernel, "add_core", 2 * HALF, sums, received.reshape(2 * HALF, 128))
+    plane = lax.all_to_all(pair.reshape(4, 384, 2, 128), "x", 0, 0, tiled=True)
+    plane = small_call(line_kernel, "add_line", 768, plane.reshape(2 * HALF, 128))
     last = lax.all_to_all(plane.reshape(64, CAP, 2, 128), ("zh", "zl", "y"), 0, 0, tiled=True)
     out = insert_call(mine, last.reshape(768, 128))
     return out.reshape(512, 2, 128).transpose(1, 0, 2).reshape(2, 65536)

time: 109 us -> 104 us (0.954)
  Pallas kernels: 21.4 us -> 18.4 us
  other arithmetic: 1.98 us -> 0 us
    pallas_call x1, Pallas kernels: 5.24 us -> 3.38 us  [pick_call(): pl.pallas_call(pick_kernel, out_shape=(shape((REFS, KY), jnp.int32), shap...]
    pallas_call x1, Pallas kernels: 12.9 us -> 11.5 us  [search_call(): pl.pallas_call(search_kernel, out_shape=(shape((4 * HALF, KX), F32), shap...]
    reduce_sum x1 -> x0, other arithmetic: 1.15 us -> none  [local(): plane = jnp.sum(plane.astype(F32), axis=0).astype(BF16)]
where the time goes in v3:
time: 104 us
  blocking collectives  77.8 us (75%)
  Pallas kernels  18.4 us (18%)
  starting transfers between devices  3.94 us (4%)
  waiting for transfers between devices  2.94 us (3%)
    all_to_all x1, blocking collectives, local(): lax.all_to_all(compact.reshape(64, CAP, 2, 128), ('zh', 'zl', 'y'), 0, 0,...  29.7 us
    all_to_all x1, blocking collectives, local(): lax.all_to_all(plane.reshape(64, CAP, 2, 128), ('zh', 'zl', 'y'), 0, 0, t...  18.4 us
    all_to_all x1, blocking collectives, local(): plane = lax.all_to_all(pair.reshape(4, 384, 2, 128), 'x', 0, 0, tiled=True)  15.3 us
    all_to_all x1, blocking collectives, local(): near = lax.all_to_all(spread, 'x', 0, 0, tiled=True).reshape(HALF, 2, 128)  14.5 us
    pallas_call x1, Pallas kernels, search_call(): pl.pallas_call(search_kernel, out_shape=(shape((4 * HALF, KX), F32), shap...  11.5 us
    pallas_call x1, Pallas kernels, pick_call(): pl.pallas_call(pick_kernel, out_shape=(shape((REFS, KY), jnp.int32), shap...  3.38 us
    ppermute x1, waiting for transfers between devices, local(): received = lax.ppermute(far_out.reshape(HALF, 2, 128), 'c', swap)  2.14 us
  transfers between devices with their start and end apart: 2, of which 2 were waited for; matrix products, arithmetic and copies ran while one was open for 0% of the time, Pallas kernels for 1%

profile of v3, /device:TPU:8, one launch (start us, length us, event | category | flops | bytes accessed | tf_op | source)
XLA Modules:
  0.0 103.7 jit_solution(6246061162191607874)
XLA Ops:
  0.0 0.0 copy-start.8
  0.0 0.0 copy-start.7
  0.0 3.4 %pick_rows.1 = (s32[8,256]{1,0:T(8,128)}, s32[8,128]{1,0:T(8,128)}, bf16[768,128]{1,0:T(8,128)(2,1)}) custom-call(s32[1]{0:T(128)} %bitcast.me_ref, s32[8,256]{1,0:T(8,128)} %own_hbm.1, bf16[1024,128]{1,0:T(8,128)(2,1)} %bitcast.36, s32[2048,128]{1,0:T(8,128)} %bitcast.34), custom_call_target="tpu_custom_call" | custom-call | tf_op jit(solution)/shard_map/pick_rows/pallas_call | solution.py:291
  3.4 29.7 %all_to_all.20 = bf16[64,6,2,128]{3,2,1,0:T(2,128)(2,1)S(1)} all-to-all(bf16[64,6,2,128]{3,2,1,0:T(2,128)(2,1)} %bitcast.37), channel_id=1, replica_groups=mesh['zh'=4,'c'=2,'y'=8,'x'=4,'zl'=2] {'zh','zl','y'}, dimensions={0} | all-to-all | bytes 393216 | tf_op jit(solution)/shard_map/all_to_all | solution.py:379
  33.1 0.4 broadcast_in_dim.8
  33.5 14.5 %all_to_all.21 = bf16[4,384,2,128]{3,2,1,0:T(2,128)(2,1)S(1)} all-to-all(bf16[4,384,2,128]{3,2,1,0:T(2,128)(2,1)S(1)} %broadcast_in_dim.8), channel_id=1, replica_groups=mesh['zh'=4,'c'=2,'y'=8,'x'=4,'zl'=2] {'x'}, dimensions={0} | all-to-all | bytes 1572864 | tf_op jit(solution)/shard_map/all_to_all | solution.py:381
  48.0 1.9 %collective-permute-start = (bf16[1536,2,128]{2,1,0:T(2,128)(2,1)S(1)}, bf16[1536,2,128]{2,1,0:T(2,128)(2,1)S(1)}, u32[]{:S(2)}, u32[]{:S(2)}) collective-permute-start(bf16[1536,2,128]{2,1,0:T(2,128)(2,1)S(1)} %bitcast.24), channel_id=1, source_target_pairs={{0,64},{64,0},{1,65},{65,1},{2,66},{66,2},{3,67},{67,3},{4,68},{68... | collective-permute-start | bytes 2359304 | tf_op jit(solution)/shard_map/ppermute | solution.py:383
  49.9 0.0 copy-done.8
  49.9 0.0 copy-done.7
  49.9 0.0 copy-start
  49.9 0.0 copy-start.1
  49.9 0.0 copy-start.2
  50.0 0.0 copy-start.3
  50.0 0.0 copy-start.4
  50.0 0.0 copy-start.6
  50.0 1.4 %ctf_images.1 = (f32[2048,128]{1,0:T(8,128)S(1)}, f32[1024,128]{1,0:T(8,128)S(1)}) custom-call(f32[4]{0:T(128)S(1)} %copy-done.8, bf16[2048,128]{1,0:T(8,128)(2,1)S(1)} %bitcast.33), custom_call_target="tpu_custom_call" | custom-call | flops 4000000000 | bytes 4000000 | tf_op jit(solution)/shard_map/ctf_images/pallas_call | solution.py:314
  51.3 0.8 collective-permute-done
  52.1 0.0 copy-done
  52.1 0.0 copy-done.1
  52.1 0.0 copy-done.2
  52.2 0.0 copy-done.3
  52.2 0.0 copy-done.4
  52.2 0.0 copy-done.6
  52.2 11.5 %shift_search.1 = (f32[6144,128]{1,0:T(8,128)S(1)}, bf16[3072,128]{1,0:T(8,128)(2,1)S(1)}) custom-call(s32[8,256]{1,0:T(8,128)S(1)} %copy-done.4, f32[4]{0:T(128)S(1)} %copy-done.6, bf16[3072,128]{1,0:T(8,128)(2,1)S(1)} %bitcast.25, bf16[3072,128]{1,0:T(8,128)(2,1)S(1)} %bitcast.28, f32[2048,128]{1,0:T(8,128)S(1)} %get-tuple-element.15.img_ref, ...), custom_call_target="tpu_custom_call" | custom-call | tf_op jit(solution)/shard_map/shift_search/pallas_call | solution.py:328
  63.7 2.0 %collective-permute-start.1 = (bf16[1536,2,128]{2,1,0:T(2,128)(2,1)S(1)}, bf16[1536,2,128]{2,1,0:T(2,128)(2,1)S(1)}, u32[]{:S(2)}, u32[]{:S(2)}) collective-permute-start(bf16[1536,2,128]{2,1,0:T(2,128)(2,1)S(1)} %bitcast.32), channel_id=1, source_target_pairs={{0,64},{64,0},{1,65},{65,1},{2,66},{66,2},{3,67},{67,3},{4,68},{68... | collective-permute-start | bytes 2359304 | tf_op jit(solution)/shard_map/ppermute | solution.py:388
  65.8 2.1 %collective-permute-done.1 = bf16[1536,2,128]{2,1,0:T(2,128)(2,1)S(1)} collective-permute-done((bf16[1536,2,128]{2,1,0:T(2,128)(2,1)S(1)}, bf16[1536,2,128]{2,1,0:T(2,128)(2,1)S(1)}, u32[]{:S(2)}, u32[]{:S(2)}) %collective-permute-start.1) | collective-permute-done | bytes 786464 | tf_op jit(solution)/shard_map/ppermute | solution.py:388
  67.9 0.0 copy-start.5
  67.9 0.2 add_core.1
  68.1 15.3 %all_to_all.22 = bf16[4,384,2,128]{3,2,1,0:T(2,128)(2,1)S(1)} all-to-all(bf16[4,384,2,128]{3,2,1,0:T(2,128)(2,1)S(1)} %bitcast.26), channel_id=1, replica_groups=mesh['zh'=4,'c'=2,'y'=8,'x'=4,'zl'=2] {'x'}, dimensions={0} | all-to-all | bytes 1572864 | tf_op jit(solution)/shard_map/all_to_all | solution.py:390
  83.4 0.1 add_line.1
  83.5 18.4 %all_to_all.23 = bf16[64,6,2,128]{3,2,1,0:T(2,128)(2,1)S(1)} all-to-all(bf16[64,6,2,128]{3,2,1,0:T(2,128)(2,1)S(1)} %bitcast.31), channel_id=1, replica_groups=mesh['zh'=4,'c'=2,'y'=8,'x'=4,'zl'=2] {'zh','zl','y'}, dimensions={0} | all-to-all | bytes 393216 | tf_op jit(solution)/shard_map/all_to_all | solution.py:392
  101.9 0.0 copy-done.5
  101.9 1.9 %insert_rows.1 = f32[1024,128]{1,0:T(8,128)} custom-call(s32[8,128]{1,0:T(8,128)S(1)} %copy-done.5, bf16[768,128]{1,0:T(8,128)(2,1)S(1)} %bitcast.30), custom_call_target="tpu_custom_call" | custom-call | tf_op jit(solution)/shard_map/insert_rows/pallas_call | solution.py:360
Async XLA Ops:
  0.0 49.9 %copy-start.8 = (f32[4]{0:T(128)S(1)}, f32[4]{0:T(128)}, u32[]{:S(2)}) copy-start(f32[4]{0:T(128)} %defocus_ref.1) | copy-start | bytes 52
  0.0 49.9 %copy-start.7 = (bf16[4,256,2,128]{3,2,1,0:T(2,128)(2,1)S(1)}, bf16[4,256,2,128]{3,2,1,0:T(2,128)(2,1)}, u32[]{:S(2)}) copy-start(bf16[4,256,2,128]{3,2,1,0:T(2,128)(2,1)} %param.10) | copy-start | bytes 1572868
  48.0 4.2 %collective-permute-start = (bf16[1536,2,128]{2,1,0:T(2,128)(2,1)S(1)}, bf16[1536,2,128]{2,1,0:T(2,128)(2,1)S(1)}, u32[]{:S(2)}, u32[]{:S(2)}) collective-permute-start(bf16[1536,2,128]{2,1,0:T(2,128)(2,1)S(1)} %bitcast.24), channel_id=1, source_target_pairs={{0,64},{64,0},{1,65},{65,1},{2,66},{66,2},{3,67},{67,3},{4,68},{68... | collective-permute-start | bytes 2359304 | tf_op jit(solution)/shard_map/ppermute | solution.py:383
  49.9 2.2 %copy-start = (bf16[256,1024]{1,0:T(8,128)(2,1)S(1)}, bf16[256,1024]{1,0:T(8,128)(2,1)}, u32[]{:S(2)}) copy-start(bf16[256,1024]{1,0:T(8,128)(2,1)} %constant.36.clone.bwd_ref) | copy-start | bytes 1572868
  49.9 2.2 %copy-start.1 = (bf16[1024,256]{1,0:T(8,128)(2,1)S(1)}, bf16[1024,256]{1,0:T(8,128)(2,1)}, u32[]{:S(2)}) copy-start(bf16[1024,256]{1,0:T(8,128)(2,1)} %constant.35.clone.fwd_ref) | copy-start | bytes 1572868
  49.9 2.2 %copy-start.2 = (bf16[512,32]{1,0:T(8,128)(2,1)S(1)}, bf16[512,32]{1,0:T(8,128)(2,1)}, u32[]{:S(2)}) copy-start(bf16[512,32]{1,0:T(8,128)(2,1)} %constant.38.clone.back_ref) | copy-start | bytes 98308
  50.0 2.2 %copy-start.3 = (bf16[64,256]{1,0:T(8,128)(2,1)S(1)}, bf16[64,256]{1,0:T(8,128)(2,1)}, u32[]{:S(2)}) copy-start(bf16[64,256]{1,0:T(8,128)(2,1)} %constant.37.clone.corr_ref) | copy-start | bytes 98308
  50.0 2.2 %copy-start.4 = (s32[8,256]{1,0:T(8,128)S(1)}, s32[8,256]{1,0:T(8,128)}, u32[]{:S(2)}) copy-start(s32[8,256]{1,0:T(8,128)} %get-tuple-element.13.pos_ref) | copy-start | bytes 24580
  50.0 2.2 %copy-start.6 = (f32[4]{0:T(128)S(1)}, f32[4]{0:T(128)}, u32[]{:S(2)}) copy-start(f32[4]{0:T(128)} %noise_ref.1) | copy-start | bytes 52
  63.7 4.2 %collective-permute-start.1 = (bf16[1536,2,128]{2,1,0:T(2,128)(2,1)S(1)}, bf16[1536,2,128]{2,1,0:T(2,128)(2,1)S(1)}, u32[]{:S(2)}, u32[]{:S(2)}) collective-permute-start(bf16[1536,2,128]{2,1,0:T(2,128)(2,1)S(1)} %bitcast.32), channel_id=1, source_target_pairs={{0,64},{64,0},{1,65},{65,1},{2,66},{66,2},{3,67},{67,3},{4,68},{68... | collective-permute-start | bytes 2359304 | tf_op jit(solution)/shard_map/ppermute | solution.py:388
  67.9 34.0 %copy-start.5 = (s32[8,128]{1,0:T(8,128)S(1)}, s32[8,128]{1,0:T(8,128)}, u32[]{:S(2)}) copy-start(s32[8,128]{1,0:T(8,128)} %get-tuple-element.12.mine_ref) | copy-start | bytes 12292

commit v4 on v3

--- a/solution.py
+++ b/solution.py
@@ -132,10 +132,12 @@
 
 
 CH = 64
+BIG = 1024
+PIECES = 2
 
 
 def search_kernel(pos_ref, noise_ref, near_ref, far_ref, img_ref, sq_ref, fwd_ref, bwd_ref, corr_ref, back_ref,
-                  sum_ref, far_out_ref, slots, rows_a, rows_b, q_a, q_b, power, corr, weight):
+                  sum_ref, far_out_ref, slots, rows_a, rows_b, q, row_phase, power, corr, weight):
     slots[0 : 2 * HALF, :] = near_ref[...].astype(F32)
     slots[2 * HALF : 4 * HALF, :] = far_ref[...].astype(F32)
 
@@ -153,7 +155,7 @@
         at = p * 512 + k * CH
         return img_ref[at : at + CH, :], img_ref[at + KY : at + KY + CH, :]
 
-    def score_ref(r, rows, q, ahead, ahead_rows):
+    def score_ref(r, rows, ahead, ahead_rows):
         sums = [jnp.zeros((8, KX), F32) for _ in range(PER)]
         for k in range(KY // CH):
             fetch(ahead, ahead_rows, k)
@@ -162,25 +164,29 @@
             mag = re * re + im * im
             for p in range(PER):
                 a_re, a_im = images(p, k)
-                q[k * CH : (k + 1) * CH, p * 256 : p * 256 + 128] = (re * a_re + im * a_im).astype(BF16)
-                q[k * CH : (k + 1) * CH, p * 256 + 128 : (p + 1) * 256] = (re * a_im - im * a_re).astype(BF16)
+                q[pl.ds(pl.multiple_of(r * KY + k * CH, CH), CH), p * 256 : p * 256 + 128] = (re * a_re + im * a_im).astype(BF16)
+                q[pl.ds(pl.multiple_of(r * KY + k * CH, CH), CH), p * 256 + 128 : (p + 1) * 256] = (re * a_im - im * a_re).astype(BF16)
                 part = sq_ref[p * KY + k * CH : p * KY + (k + 1) * CH, :] * mag
                 sums[p] = sums[p] + jnp.sum(part.reshape(CH // 8, 8, KX), axis=0)
         for p in range(PER):
             power[pl.ds(p * REFS + r, 1), :] = jnp.sum(sums[p], axis=0, keepdims=True)
-        row_phase = jnp.dot(q[...], fwd_ref[...], preferred_element_type=F32).astype(BF16)
-        both = jnp.dot(corr_ref[...], row_phase, preferred_element_type=F32)
-        corr[pl.ds(pl.multiple_of(r * SHIFTS, SHIFTS), SHIFTS), :] = both[:SHIFTS, :128] - both[SHIFTS:, 128:]
 
     def forward(t, carry):
         r = 2 * t
-        score_ref(r, rows_a, q_a, r + 1, rows_b)
-        score_ref(r + 1, rows_b, q_b, jnp.minimum(r + 2, REFS - 1), rows_a)
+        score_ref(r, rows_a, r + 1, rows_b)
+        score_ref(r + 1, rows_b, jnp.minimum(r + 2, REFS - 1), rows_a)
         return carry
 
     for k in range(KY // CH):
         fetch(0, rows_a, k)
     lax.fori_loop(0, REFS // 2, forward, 0)
+    for m in range(ROWS // BIG):
+        at = slice(m * BIG, (m + 1) * BIG)
+        row_phase[at, :] = jnp.dot(q[at, :], fwd_ref[...], preferred_element_type=F32).astype(BF16)
+    for r in range(REFS):
+        both = jnp.dot(corr_ref[...], row_phase[r * KY : (r + 1) * KY, :], preferred_element_type=F32)
+        corr[r * SHIFTS : (r + 1) * SHIFTS, :] = both[:SHIFTS, :128] - both[SHIFTS:, 128:]
+
 
     group = lax.shift_right_logical(iota((1, 128), 1), 5)
     noise = jnp.zeros((1, 128), F32)
@@ -235,28 +241,36 @@
     far_out_ref[...] = sum_ref[2 * HALF : 4 * HALF, :].astype(BF16)
 
 
-def insert_kernel(mine_ref, got_ref, out_ref, wide, left, right):
+def insert_kernel(mine_ref, got_ref, out_hbm, wide, left, right, out, sems):
+    hi_iota = iota((512, 128), 0)
+    lo_iota = iota((128, 128), 0)
     sums = jnp.sum(got_ref[...].astype(F32).reshape(32, 24, 128), axis=0)
     wide[...] = sums * (1.0 / math.sqrt(PARTICLES))
-    hi_iota = iota((512, 128), 0)
-    lo_iota = iota((128, 128), 0)
     for k in range(CAP):
         vox = mine_ref[k : k + 1, :]
-        hi = lax.shift_right_arithmetic(vox, 7)
-        onehot = (lo_iota == (vox & 127)).astype(F32).astype(BF16)
-        right[:, 2 * k * 128 : (2 * k + 1) * 128] = onehot
-        right[:, (2 * k + 1) * 128 : (2 * k + 2) * 128] = onehot
-        at = hi_iota == hi
+        at = slice(k * 128, (k + 1) * 128)
+        left[:, at] = (hi_iota == lax.shift_right_arithmetic(vox, 7)).astype(F32).astype(BF16)
+        here = lo_iota == (vox & 127)
         for c in range(2):
             total = wide[2 * k + c : 2 * k + c + 1, :] + wide[12 + 2 * k + c : 12 + 2 * k + c + 1, :]
             first = total.astype(BF16).astype(F32)
-            rest = total - first
-            left[c, :, 2 * k * 128 : (2 * k + 1) * 128] = jnp.where(at, first, 0.0).astype(BF16)
-            left[c, :, (2 * k + 1) * 128 : (2 * k + 2) * 128] = jnp.where(at, rest, 0.0).astype(BF16)
-    for c in range(2):
-        out_ref[pl.ds(c, 512, stride=2), :] = lax.dot_general(
-            left[c], right[...], (((1,), (1,)), ((), ())), preferred_element_type=F32
+            right[c * 256 : c * 256 + 128, at] = jnp.where(here, first, 0.0).astype(BF16)
+            right[c * 256 + 128 : c * 256 + 256, at] = jnp.where(here, total - first, 0.0).astype(BF16)
+    size = 512 // PIECES
+    stores = []
+    for m in range(PIECES):
+        both = lax.dot_general(
+            left[m * size : (m + 1) * size, :], right[...], (((1,), (1,)), ((), ())), preferred_element_type=F32
         )
+        for c in range(2):
+            out[pl.ds(2 * size * m + c, size, stride=2), :] = (
+                both[:, c * 256 : c * 256 + 128] + both[:, c * 256 + 128 : c * 256 + 256]
+            )
+        at = pl.ds(2 * size * m, 2 * size)
+        stores.append(pltpu.make_async_copy(out.at[at, :], out_hbm.at[at, :], sems.at[m]))
+        stores[m].start()
+    for store in stores:
+        store.wait()
 
 
 def pair_kernel(sums_ref, got_ref, out_ref):
@@ -305,7 +319,7 @@
             pltpu.VMEM((ROWS, KX), jnp.int32),
             pltpu.SemaphoreType.DMA((3,)),
         ],
-        compiler_params=pltpu.CompilerParams(vmem_limit_bytes=60 * 1024 * 1024),
+        compiler_params=pltpu.CompilerParams(vmem_limit_bytes=107 * 512 * 1024),
         name="pick_rows",
     )(me, owner, volume_rows, voxel_rows)
 
@@ -334,8 +348,8 @@
             pltpu.VMEM((4 * HALF, KX), F32),
             pltpu.VMEM((2 * KY, KX), F32),
             pltpu.VMEM((2 * KY, KX), F32),
-            pltpu.VMEM((KY, PER * 2 * KX), BF16),
-            pltpu.VMEM((KY, PER * 2 * KX), BF16),
+            pltpu.VMEM((REFS * KY, PER * 2 * KX), BF16),
+            pltpu.VMEM((REFS * KY, 2 * PER * SHIFTS), BF16),
             pltpu.VMEM((PER * REFS, KX), F32),
             pltpu.VMEM((REFS * SHIFTS, 128), F32),
             pltpu.VMEM((REFS * SHIFTS, 128), BF16),
@@ -361,11 +375,13 @@
         insert_kernel,
         out_shape=shape((1024, 128), F32),
         in_specs=[VM, VM],
-        out_specs=VM,
+        out_specs=ANY,
         scratch_shapes=[
             pltpu.VMEM((24, 128), F32),
-            pltpu.VMEM((2, 512, 2 * CAP * 128), BF16),
-            pltpu.VMEM((128, 2 * CAP * 128), BF16),
+            pltpu.VMEM((512, CAP * 128), BF16),
+            pltpu.VMEM((512, CAP * 128), BF16),
+            pltpu.VMEM((1024, 128), F32),
+            pltpu.SemaphoreType.DMA((PIECES,)),
         ],
         compiler_params=params(),
         name="insert_rows",

time: 104 us -> 102 us (0.981)
  Pallas kernels: 18.4 us -> 16 us
    pallas_call x1, Pallas kernels: 3.38 us -> 1.97 us  [pick_call(): pl.pallas_call(pick_kernel, out_shape=(shape((REFS, KY), jnp.int32), shap...]
where the time goes in v4:
time: 102 us
  blocking collectives  77.6 us (76%)
  Pallas kernels  16 us (16%)
  starting transfers between devices  3.94 us (4%)
  waiting for transfers between devices  2.94 us (3%)
  local copies, waits for them, and re-layouts  1.16 us (1%)
    all_to_all x1, blocking collectives, local(): lax.all_to_all(compact.reshape(64, CAP, 2, 128), ('zh', 'zl', 'y'), 0, 0,...  29.5 us
    all_to_all x1, blocking collectives, local(): lax.all_to_all(plane.reshape(64, CAP, 2, 128), ('zh', 'zl', 'y'), 0, 0, t...  18.4 us
    all_to_all x1, blocking collectives, local(): plane = lax.all_to_all(pair.reshape(4, 384, 2, 128), 'x', 0, 0, tiled=True)  15.3 us
    all_to_all x1, blocking collectives, local(): near = lax.all_to_all(spread, 'x', 0, 0, tiled=True).reshape(HALF, 2, 128)  14.5 us
    pallas_call x1, Pallas kernels, search_call(): pl.pallas_call(search_kernel, out_shape=(shape((4 * HALF, KX), F32), shap...  11 us
    ppermute x1, waiting for transfers between devices, local(): received = lax.ppermute(far_out.reshape(HALF, 2, 128), 'c', swap)  2.14 us
  transfers between devices with their start and end apart: 2, of which 2 were waited for; matrix products, arithmetic and copies ran while one was open for 0% of the time, Pallas kernels for 1%

profile of v4, /device:TPU:8, one launch (start us, length us, event | category | flops | bytes accessed | tf_op | source)
XLA Modules:
  0.0 101.8 jit_solution(1557174047879909880)
XLA Ops:
  0.0 0.0 copy-start.7
  0.0 0.0 copy-start.4
  0.0 0.7 copy-done.4
  0.7 0.0 copy-start.6
  0.7 2.0 %pick_rows.1 = (s32[8,256]{1,0:T(8,128)S(1)}, s32[8,128]{1,0:T(8,128)S(1)}, bf16[768,128]{1,0:T(8,128)(2,1)S(1)}) custom-call(s32[1]{0:T(128)} %bitcast.me_ref, s32[8,256]{1,0:T(8,128)S(1)} %copy-done.4, bf16[1024,128]{1,0:T(8,128)(2,1)} %bitcast.37, s32[2048,128]{1,0:T(8,128)} %bitcast.35), custom_call_target="tpu_custom_call" | custom-call | tf_op jit(solution)/shard_map/pick_rows/pallas_call | solution.py:305
  2.7 29.5 %all_to_all.20 = bf16[64,6,2,128]{3,2,1,0:T(2,128)(2,1)S(1)} all-to-all(bf16[64,6,2,128]{3,2,1,0:T(2,128)(2,1)S(1)} %bitcast.32), channel_id=1, replica_groups=mesh['zh'=4,'c'=2,'y'=8,'x'=4,'zl'=2] {'zh','zl','y'}, dimensions={0} | all-to-all | bytes 393216 | tf_op jit(solution)/shard_map/all_to_all | solution.py:395
  32.2 0.4 broadcast_in_dim.8
  32.6 14.5 %all_to_all.21 = bf16[4,384,2,128]{3,2,1,0:T(2,128)(2,1)S(1)} all-to-all(bf16[4,384,2,128]{3,2,1,0:T(2,128)(2,1)S(1)} %broadcast_in_dim.8), channel_id=1, replica_groups=mesh['zh'=4,'c'=2,'y'=8,'x'=4,'zl'=2] {'x'}, dimensions={0} | all-to-all | bytes 1572864 | tf_op jit(solution)/shard_map/all_to_all | solution.py:397
  47.1 1.9 %collective-permute-start = (bf16[1536,2,128]{2,1,0:T(2,128)(2,1)S(1)}, bf16[1536,2,128]{2,1,0:T(2,128)(2,1)S(1)}, u32[]{:S(2)}, u32[]{:S(2)}) collective-permute-start(bf16[1536,2,128]{2,1,0:T(2,128)(2,1)S(1)} %bitcast.24), channel_id=1, source_target_pairs={{0,64},{64,0},{1,65},{65,1},{2,66},{66,2},{3,67},{67,3},{4,68},{68... | collective-permute-start | bytes 2359304 | tf_op jit(solution)/shard_map/ppermute | solution.py:399
  49.0 0.0 copy-done.7
  49.0 0.0 copy-done.6
  49.0 0.0 copy-start
  49.0 0.0 copy-start.1
  49.0 0.0 copy-start.2
  49.0 0.0 copy-start.3
  49.1 0.0 copy-start.5
  49.1 1.4 %ctf_images.1 = (f32[2048,128]{1,0:T(8,128)S(1)}, f32[1024,128]{1,0:T(8,128)S(1)}) custom-call(f32[4]{0:T(128)S(1)} %copy-done.7, bf16[2048,128]{1,0:T(8,128)(2,1)S(1)} %bitcast.34), custom_call_target="tpu_custom_call" | custom-call | flops 4000000000 | bytes 4000000 | tf_op jit(solution)/shard_map/ctf_images/pallas_call | solution.py:328
  50.4 0.8 collective-permute-done
  51.2 0.0 copy-done
  51.2 0.0 copy-done.1
  51.2 0.0 copy-done.2
  51.2 0.0 copy-done.3
  51.3 0.0 copy-done.5
  51.3 11.0 %shift_search.1 = (f32[6144,128]{1,0:T(8,128)S(1)}, bf16[3072,128]{1,0:T(8,128)(2,1)S(1)}) custom-call(s32[8,256]{1,0:T(8,128)S(1)} %get-tuple-element.13.pos_ref, f32[4]{0:T(128)S(1)} %copy-done.5, bf16[3072,128]{1,0:T(8,128)(2,1)S(1)} %bitcast.25, bf16[3072,128]{1,0:T(8,128)(2,1)S(1)} %bitcast.28, f32[2048,128]{1,0:T(8,128)S(1)} %get-tuple-element.15.img_ref, ...), custom_call_target="tpu_custom_call" | custom-call | tf_op jit(solution)/shard_map/shift_search/pallas_call | solution.py:342
  62.2 2.0 %collective-permute-start.1 = (bf16[1536,2,128]{2,1,0:T(2,128)(2,1)S(1)}, bf16[1536,2,128]{2,1,0:T(2,128)(2,1)S(1)}, u32[]{:S(2)}, u32[]{:S(2)}) collective-permute-start(bf16[1536,2,128]{2,1,0:T(2,128)(2,1)S(1)} %bitcast.33), channel_id=1, source_target_pairs={{0,64},{64,0},{1,65},{65,1},{2,66},{66,2},{3,67},{67,3},{4,68},{68... | collective-permute-start | bytes 2359304 | tf_op jit(solution)/shard_map/ppermute | solution.py:404
  64.3 2.1 %collective-permute-done.1 = bf16[1536,2,128]{2,1,0:T(2,128)(2,1)S(1)} collective-permute-done((bf16[1536,2,128]{2,1,0:T(2,128)(2,1)S(1)}, bf16[1536,2,128]{2,1,0:T(2,128)(2,1)S(1)}, u32[]{:S(2)}, u32[]{:S(2)}) %collective-permute-start.1) | collective-permute-done | bytes 786464 | tf_op jit(solution)/shard_map/ppermute | solution.py:404
  66.4 0.2 add_core.1
  66.6 15.3 %all_to_all.22 = bf16[4,384,2,128]{3,2,1,0:T(2,128)(2,1)S(1)} all-to-all(bf16[4,384,2,128]{3,2,1,0:T(2,128)(2,1)S(1)} %bitcast.26), channel_id=1, replica_groups=mesh['zh'=4,'c'=2,'y'=8,'x'=4,'zl'=2] {'x'}, dimensions={0} | all-to-all | bytes 1572864 | tf_op jit(solution)/shard_map/all_to_all | solution.py:406
  81.9 0.1 add_line.1
  82.0 18.4 %all_to_all.23 = bf16[64,6,2,128]{3,2,1,0:T(2,128)(2,1)S(1)} all-to-all(bf16[64,6,2,128]{3,2,1,0:T(2,128)(2,1)S(1)} %bitcast.31), channel_id=1, replica_groups=mesh['zh'=4,'c'=2,'y'=8,'x'=4,'zl'=2] {'zh','zl','y'}, dimensions={0} | all-to-all | bytes 393216 | tf_op jit(solution)/shard_map/all_to_all | solution.py:408
  100.4 1.4 %insert_rows.1 = f32[1024,128]{1,0:T(8,128)} custom-call(s32[8,128]{1,0:T(8,128)S(1)} %get-tuple-element.12.mine_ref, bf16[768,128]{1,0:T(8,128)(2,1)S(1)} %bitcast.30), custom_call_target="tpu_custom_call" | custom-call | tf_op jit(solution)/shard_map/insert_rows/pallas_call | solution.py:374
Async XLA Ops:
  0.0 49.0 %copy-start.7 = (f32[4]{0:T(128)S(1)}, f32[4]{0:T(128)}, u32[]{:S(2)}) copy-start(f32[4]{0:T(128)} %defocus_ref.1) | copy-start | bytes 52
  0.0 0.7 copy-start.4
  0.7 48.3 %copy-start.6 = (bf16[4,256,2,128]{3,2,1,0:T(2,128)(2,1)S(1)}, bf16[4,256,2,128]{3,2,1,0:T(2,128)(2,1)}, u32[]{:S(2)}) copy-start(bf16[4,256,2,128]{3,2,1,0:T(2,128)(2,1)} %param.10) | copy-start | bytes 1572868
  47.1 4.2 %collective-permute-start = (bf16[1536,2,128]{2,1,0:T(2,128)(2,1)S(1)}, bf16[1536,2,128]{2,1,0:T(2,128)(2,1)S(1)}, u32[]{:S(2)}, u32[]{:S(2)}) collective-permute-start(bf16[1536,2,128]{2,1,0:T(2,128)(2,1)S(1)} %bitcast.24), channel_id=1, source_target_pairs={{0,64},{64,0},{1,65},{65,1},{2,66},{66,2},{3,67},{67,3},{4,68},{68... | collective-permute-start | bytes 2359304 | tf_op jit(solution)/shard_map/ppermute | solution.py:399
  49.0 2.2 %copy-start = (bf16[256,1024]{1,0:T(8,128)(2,1)S(1)}, bf16[256,1024]{1,0:T(8,128)(2,1)}, u32[]{:S(2)}) copy-start(bf16[256,1024]{1,0:T(8,128)(2,1)} %constant.36.clone.bwd_ref) | copy-start | bytes 1572868
  49.0 2.2 %copy-start.1 = (bf16[1024,256]{1,0:T(8,128)(2,1)S(1)}, bf16[1024,256]{1,0:T(8,128)(2,1)}, u32[]{:S(2)}) copy-start(bf16[1024,256]{1,0:T(8,128)(2,1)} %constant.35.clone.fwd_ref) | copy-start | bytes 1572868
  49.0 2.2 %copy-start.2 = (bf16[512,32]{1,0:T(8,128)(2,1)S(1)}, bf16[512,32]{1,0:T(8,128)(2,1)}, u32[]{:S(2)}) copy-start(bf16[512,32]{1,0:T(8,128)(2,1)} %constant.38.clone.back_ref) | copy-start | bytes 98308
  49.0 2.2 %copy-start.3 = (bf16[64,256]{1,0:T(8,128)(2,1)S(1)}, bf16[64,256]{1,0:T(8,128)(2,1)}, u32[]{:S(2)}) copy-start(bf16[64,256]{1,0:T(8,128)(2,1)} %constant.37.clone.corr_ref) | copy-start | bytes 98308
  49.1 2.2 %copy-start.5 = (f32[4]{0:T(128)S(1)}, f32[4]{0:T(128)}, u32[]{:S(2)}) copy-start(f32[4]{0:T(128)} %noise_ref.1) | copy-start | bytes 52
  62.2 4.2 %collective-permute-start.1 = (bf16[1536,2,128]{2,1,0:T(2,128)(2,1)S(1)}, bf16[1536,2,128]{2,1,0:T(2,128)(2,1)S(1)}, u32[]{:S(2)}, u32[]{:S(2)}) collective-permute-start(bf16[1536,2,128]{2,1,0:T(2,128)(2,1)S(1)} %bitcast.33), channel_id=1, source_target_pairs={{0,64},{64,0},{1,65},{65,1},{2,66},{66,2},{3,67},{67,3},{4,68},{68... | collective-permute-start | bytes 2359304 | tf_op jit(solution)/shard_map/ppermute | solution.py:404

commit v5 on v4

--- a/solution.py
+++ b/solution.py
@@ -75,11 +75,11 @@
     row_id = iota((REFS, KY), 0) * KY + iota((REFS, KY), 1)
     is_me = own == me
     found = [jnp.max(jnp.where(is_me & (slots == k), row_id, -1)) for k in range(CAP)]
-    z = lax.shift_right_logical(own, 7) * 2 + (own & 1)
+    z = lax.shift_right_logical(own, 7)
     y = lax.shift_right_logical(own, 3) & 7
     x = lax.shift_right_logical(own, 1) & 3
     across = ((lax.shift_right_logical(own, 6) ^ lax.shift_right_logical(me, 6)) & 1) * HALF
-    pos_ref[...] = 2 * (across + x * (64 * CAP) + (z * 8 + y) * CAP + jnp.minimum(slots, CAP - 1))
+    pos_ref[...] = 2 * (across + (x * 2 + (own & 1)) * (32 * CAP) + (z * 8 + y) * CAP + jnp.minimum(slots, CAP - 1))
     parity = (iota((8, 128), 0) & 1) == 0
     row_pair = lax.shift_right_logical(iota((1024, 128), 0), 1)
     lo_iota = iota((128, 128), 0)
@@ -101,7 +101,7 @@
             stage[copy * 12 + 2 * k : copy * 12 + 2 * k + 1, :] = re
             stage[copy * 12 + 2 * k + 1 : copy * 12 + 2 * k + 2, :] = im
     block = stage[...].astype(BF16)
-    for copy in range(8):
+    for copy in range(4):
         out_ref[copy * 96 : (copy + 1) * 96, :] = block
 
 
@@ -244,7 +244,7 @@
 def insert_kernel(mine_ref, got_ref, out_hbm, wide, left, right, out, sems):
     hi_iota = iota((512, 128), 0)
     lo_iota = iota((128, 128), 0)
-    sums = jnp.sum(got_ref[...].astype(F32).reshape(32, 24, 128), axis=0)
+    sums = jnp.sum(got_ref[...].astype(F32).reshape(16, 24, 128), axis=0)
     wide[...] = sums * (1.0 / math.sqrt(PARTICLES))
     for k in range(CAP):
         vox = mine_ref[k : k + 1, :]
@@ -278,9 +278,9 @@
 
 
 def line_kernel(got_ref, out_ref):
-    total = got_ref[0:768, :].astype(F32)
-    for k in range(1, 4):
-        total = total + got_ref[k * 768 : (k + 1) * 768, :].astype(F32)
+    total = got_ref[0:384, :].astype(F32)
+    for k in range(1, 8):
+        total = total + got_ref[k * 384 : (k + 1) * 384, :].astype(F32)
     out_ref[...] = total.astype(BF16)
 
 
@@ -307,7 +307,7 @@
         out_shape=(
             shape((REFS, KY), jnp.int32),
             shape((8, 128), jnp.int32),
-            shape((64 * 12, 128), BF16),
+            shape((32 * 12, 128), BF16),
         ),
         in_specs=[SM, ANY, ANY, ANY],
         out_specs=(VM, VM, VM),
@@ -392,9 +392,9 @@
     me = lax.axis_index(FINE).astype(jnp.int32).reshape(1)
     volume_rows = volume.reshape(2, 512, 128).transpose(1, 0, 2).reshape(1024, 128)
     pos, mine, compact = pick_call(me, slice_owner, volume_rows, slice_voxel.reshape(ROWS, KX))
-    line = lax.all_to_all(compact.reshape(64, CAP, 2, 128), ("zh", "zl", "y"), 0, 0, tiled=True)
-    spread = jnp.broadcast_to(line.reshape(1, 384, 2, 128), (4, 384, 2, 128))
-    near = lax.all_to_all(spread, "x", 0, 0, tiled=True).reshape(HALF, 2, 128)
+    line = lax.all_to_all(compact.reshape(32, CAP, 2, 128), ("zh", "y"), 0, 0, tiled=True)
+    spread = jnp.broadcast_to(line.reshape(1, 192, 2, 128), (8, 192, 2, 128))
+    near = lax.all_to_all(spread, ("x", "zl"), 0, 0, tiled=True).reshape(HALF, 2, 128)
     swap = [(0, 1), (1, 0)]
     far = lax.ppermute(near, "c", swap)
     img, sq = image_call(defocus, particles.reshape(PER * KY * 2, KX))
@@ -403,10 +403,10 @@
     )
     received = lax.ppermute(far_out.reshape(HALF, 2, 128), "c", swap)
     pair = small_call(pair_kernel, "add_core", 2 * HALF, sums, received.reshape(2 * HALF, 128))
-    plane = lax.all_to_all(pair.reshape(4, 384, 2, 128), "x", 0, 0, tiled=True)
-    plane = small_call(line_kernel, "add_line", 768, plane.reshape(2 * HALF, 128))
-    last = lax.all_to_all(plane.reshape(64, CAP, 2, 128), ("zh", "zl", "y"), 0, 0, tiled=True)
-    out = insert_call(mine, last.reshape(768, 128))
+    plane = lax.all_to_all(pair.reshape(8, 192, 2, 128), ("x", "zl"), 0, 0, tiled=True)
+    plane = small_call(line_kernel, "add_line", 384, plane.reshape(2 * HALF, 128))
+    last = lax.all_to_all(plane.reshape(32, CAP, 2, 128), ("zh", "y"), 0, 0, tiled=True)
+    out = insert_call(mine, last.reshape(384, 128))
     return out.reshape(512, 2, 128).transpose(1, 0, 2).reshape(2, 65536)
 
 

time: 102 us -> 101 us (level)
  blocking collectives: 77.6 us -> 75.8 us
    all_to_all x4, blocking collectives: 77.6 us -> 75.8 us  [the longest x1 27.8 us: local(): lax.all_to_all(compact.reshape(32, CAP, 2, 128), ('zh', 'y'), 0, 0, tiled...]
where the time goes in v5:
time: 101 us
  blocking collectives  75.8 us (75%)
  Pallas kernels  16 us (16%)
  starting transfers between devices  3.94 us (4%)
  waiting for transfers between devices  2.95 us (3%)
  local copies, waits for them, and re-layouts  2.11 us (2%)
    all_to_all x1, blocking collectives, local(): lax.all_to_all(compact.reshape(32, CAP, 2, 128), ('zh', 'y'), 0, 0, tiled...  27.8 us
    all_to_all x1, blocking collectives, local(): lax.all_to_all(spread, ('x', 'zl'), 0, 0, tiled=True).reshape(HALF, 2, 128)  16.6 us
    all_to_all x1, blocking collectives, local(): lax.all_to_all(pair.reshape(8, 192, 2, 128), ('x', 'zl'), 0, 0, tiled=True)  15.9 us
    all_to_all x1, blocking collectives, local(): lax.all_to_all(plane.reshape(32, CAP, 2, 128), ('zh', 'y'), 0, 0, tiled=T...  15.6 us
    pallas_call x1, Pallas kernels, search_call(): pl.pallas_call(search_kernel, out_shape=(shape((4 * HALF, KX), F32), shap...  11 us
    ppermute x1, waiting for transfers between devices, local(): received = lax.ppermute(far_out.reshape(HALF, 2, 128), 'c', swap)  2.14 us
    ppermute x1, starting transfers between devices, local(): received = lax.ppermute(far_out.reshape(HALF, 2, 128), 'c', swap)  2.03 us
  transfers between devices with their start and end apart: 2, of which 2 were waited for; matrix products, arithmetic and copies ran while one was open for 0% of the time, Pallas kernels for 1%

profile of v5, /device:TPU:8, one launch (start us, length us, event | category | flops | bytes accessed | tf_op | source)
XLA Modules:
  0.0 101.0 jit_solution(8884916452302271270)
XLA Ops:
  0.0 0.0 copy-start.8
  0.0 0.0 copy-start.2
  0.0 1.0 copy-done.2
  1.0 0.0 copy-start.5
  1.0 0.7 copy-done.5
  1.7 0.0 copy-start.7
  1.7 2.0 %pick_rows.1 = (s32[8,256]{1,0:T(8,128)S(1)}, s32[8,128]{1,0:T(8,128)S(1)}, bf16[384,128]{1,0:T(8,128)(2,1)S(1)}) custom-call(s32[1]{0:T(128)} %bitcast.me_ref, s32[8,256]{1,0:T(8,128)S(1)} %copy-done.5, bf16[1024,128]{1,0:T(8,128)(2,1)S(1)} %bitcast.32, s32[2048,128]{1,0:T(8,128)} %bitcast.36), custom_call_target="tpu_custom_call" | custom-call | tf_op jit(solution)/shard_map/pick_rows/pallas_call | solution.py:305
  3.6 27.8 %all_to_all.20 = bf16[32,6,2,128]{3,2,1,0:T(2,128)(2,1)S(1)} all-to-all(bf16[32,6,2,128]{3,2,1,0:T(2,128)(2,1)S(1)} %bitcast.33), channel_id=1, replica_groups=mesh['zh'=4,'c'=2,'y'=8,'x'=4,'zl'=2] {'zh','y'}, dimensions={0} | all-to-all | bytes 196608 | tf_op jit(solution)/shard_map/all_to_all | solution.py:395
  31.4 0.4 broadcast_in_dim.8
  31.8 16.6 %all_to_all.21 = bf16[8,192,2,128]{3,2,1,0:T(2,128)(2,1)S(1)} all-to-all(bf16[8,192,2,128]{3,2,1,0:T(2,128)(2,1)S(1)} %broadcast_in_dim.8), channel_id=1, replica_groups=mesh['zh'=4,'c'=2,'y'=8,'x'=4,'zl'=2] {'x','zl'}, dimensions={0} | all-to-all | bytes 1572864 | tf_op jit(solution)/shard_map/all_to_all | solution.py:397
  48.4 1.9 %collective-permute-start = (bf16[1536,2,128]{2,1,0:T(2,128)(2,1)S(1)}, bf16[1536,2,128]{2,1,0:T(2,128)(2,1)S(1)}, u32[]{:S(2)}, u32[]{:S(2)}) collective-permute-start(bf16[1536,2,128]{2,1,0:T(2,128)(2,1)S(1)} %bitcast.24), channel_id=1, source_target_pairs={{0,64},{64,0},{1,65},{65,1},{2,66},{66,2},{3,67},{67,3},{4,68},{68... | collective-permute-start | bytes 2359304 | tf_op jit(solution)/shard_map/ppermute | solution.py:399
  50.3 0.0 copy-done.8
  50.3 0.0 copy-done.7
  50.3 0.0 copy-start
  50.3 0.0 copy-start.1
  50.3 0.0 copy-start.3
  50.3 0.0 copy-start.4
  50.4 0.0 copy-start.6
  50.4 1.4 %ctf_images.1 = (f32[2048,128]{1,0:T(8,128)S(1)}, f32[1024,128]{1,0:T(8,128)S(1)}) custom-call(f32[4]{0:T(128)S(1)} %copy-done.8, bf16[2048,128]{1,0:T(8,128)(2,1)S(1)} %bitcast.35), custom_call_target="tpu_custom_call" | custom-call | flops 4000000000 | bytes 4000000 | tf_op jit(solution)/shard_map/ctf_images/pallas_call | solution.py:328
  51.7 0.8 collective-permute-done
  52.5 0.0 copy-done
  52.5 0.0 copy-done.1
  52.5 0.0 copy-done.3
  52.6 0.0 copy-done.4
  52.6 0.0 copy-done.6
  52.6 11.0 %shift_search.1 = (f32[6144,128]{1,0:T(8,128)S(1)}, bf16[3072,128]{1,0:T(8,128)(2,1)S(1)}) custom-call(s32[8,256]{1,0:T(8,128)S(1)} %get-tuple-element.13.pos_ref, f32[4]{0:T(128)S(1)} %copy-done.6, bf16[3072,128]{1,0:T(8,128)(2,1)S(1)} %bitcast.25, bf16[3072,128]{1,0:T(8,128)(2,1)S(1)} %bitcast.28, f32[2048,128]{1,0:T(8,128)S(1)} %get-tuple-element.15.img_ref, ...), custom_call_target="tpu_custom_call" | custom-call | tf_op jit(solution)/shard_map/shift_search/pallas_call | solution.py:342
  63.5 2.0 %collective-permute-start.1 = (bf16[1536,2,128]{2,1,0:T(2,128)(2,1)S(1)}, bf16[1536,2,128]{2,1,0:T(2,128)(2,1)S(1)}, u32[]{:S(2)}, u32[]{:S(2)}) collective-permute-start(bf16[1536,2,128]{2,1,0:T(2,128)(2,1)S(1)} %bitcast.34), channel_id=1, source_target_pairs={{0,64},{64,0},{1,65},{65,1},{2,66},{66,2},{3,67},{67,3},{4,68},{68... | collective-permute-start | bytes 2359304 | tf_op jit(solution)/shard_map/ppermute | solution.py:404
  65.6 2.1 %collective-permute-done.1 = bf16[1536,2,128]{2,1,0:T(2,128)(2,1)S(1)} collective-permute-done((bf16[1536,2,128]{2,1,0:T(2,128)(2,1)S(1)}, bf16[1536,2,128]{2,1,0:T(2,128)(2,1)S(1)}, u32[]{:S(2)}, u32[]{:S(2)}) %collective-permute-start.1) | collective-permute-done | bytes 786464 | tf_op jit(solution)/shard_map/ppermute | solution.py:404
  67.7 0.2 add_core.1
  67.9 15.9 %all_to_all.22 = bf16[8,192,2,128]{3,2,1,0:T(2,128)(2,1)S(1)} all-to-all(bf16[8,192,2,128]{3,2,1,0:T(2,128)(2,1)S(1)} %bitcast.26), channel_id=1, replica_groups=mesh['zh'=4,'c'=2,'y'=8,'x'=4,'zl'=2] {'x','zl'}, dimensions={0} | all-to-all | bytes 1572864 | tf_op jit(solution)/shard_map/all_to_all | solution.py:406
  83.8 0.1 add_line.1
  83.9 15.6 %all_to_all.23 = bf16[32,6,2,128]{3,2,1,0:T(2,128)(2,1)S(1)} all-to-all(bf16[32,6,2,128]{3,2,1,0:T(2,128)(2,1)S(1)} %bitcast.31), channel_id=1, replica_groups=mesh['zh'=4,'c'=2,'y'=8,'x'=4,'zl'=2] {'zh','y'}, dimensions={0} | all-to-all | bytes 196608 | tf_op jit(solution)/shard_map/all_to_all | solution.py:408
  99.5 1.4 %insert_rows.1 = f32[1024,128]{1,0:T(8,128)} custom-call(s32[8,128]{1,0:T(8,128)S(1)} %get-tuple-element.12.mine_ref, bf16[384,128]{1,0:T(8,128)(2,1)S(1)} %bitcast.30), custom_call_target="tpu_custom_call" | custom-call | tf_op jit(solution)/shard_map/insert_rows/pallas_call | solution.py:374
Async XLA Ops:
  0.0 50.3 %copy-start.8 = (f32[4]{0:T(128)S(1)}, f32[4]{0:T(128)}, u32[]{:S(2)}) copy-start(f32[4]{0:T(128)} %defocus_ref.1) | copy-start | bytes 52
  0.0 1.0 copy-start.2
  1.0 0.7 copy-start.5
  1.7 48.6 %copy-start.7 = (bf16[4,256,2,128]{3,2,1,0:T(2,128)(2,1)S(1)}, bf16[4,256,2,128]{3,2,1,0:T(2,128)(2,1)}, u32[]{:S(2)}) copy-start(bf16[4,256,2,128]{3,2,1,0:T(2,128)(2,1)} %param.10) | copy-start | bytes 1572868
  48.4 4.2 %collective-permute-start = (bf16[1536,2,128]{2,1,0:T(2,128)(2,1)S(1)}, bf16[1536,2,128]{2,1,0:T(2,128)(2,1)S(1)}, u32[]{:S(2)}, u32[]{:S(2)}) collective-permute-start(bf16[1536,2,128]{2,1,0:T(2,128)(2,1)S(1)} %bitcast.24), channel_id=1, source_target_pairs={{0,64},{64,0},{1,65},{65,1},{2,66},{66,2},{3,67},{67,3},{4,68},{68... | collective-permute-start | bytes 2359304 | tf_op jit(solution)/shard_map/ppermute | solution.py:399
  50.3 2.2 %copy-start = (bf16[256,1024]{1,0:T(8,128)(2,1)S(1)}, bf16[256,1024]{1,0:T(8,128)(2,1)}, u32[]{:S(2)}) copy-start(bf16[256,1024]{1,0:T(8,128)(2,1)} %constant.36.clone.bwd_ref) | copy-start | bytes 1572868
  50.3 2.2 %copy-start.1 = (bf16[1024,256]{1,0:T(8,128)(2,1)S(1)}, bf16[1024,256]{1,0:T(8,128)(2,1)}, u32[]{:S(2)}) copy-start(bf16[1024,256]{1,0:T(8,128)(2,1)} %constant.35.clone.fwd_ref) | copy-start | bytes 1572868
  50.3 2.2 %copy-start.3 = (bf16[512,32]{1,0:T(8,128)(2,1)S(1)}, bf16[512,32]{1,0:T(8,128)(2,1)}, u32[]{:S(2)}) copy-start(bf16[512,32]{1,0:T(8,128)(2,1)} %constant.38.clone.back_ref) | copy-start | bytes 98308
  50.3 2.2 %copy-start.4 = (bf16[64,256]{1,0:T(8,128)(2,1)S(1)}, bf16[64,256]{1,0:T(8,128)(2,1)}, u32[]{:S(2)}) copy-start(bf16[64,256]{1,0:T(8,128)(2,1)} %constant.37.clone.corr_ref) | copy-start | bytes 98308
  50.4 2.2 %copy-start.6 = (f32[4]{0:T(128)S(1)}, f32[4]{0:T(128)}, u32[]{:S(2)}) copy-start(f32[4]{0:T(128)} %noise_ref.1) | copy-start | bytes 52
  63.5 4.2 %collective-permute-start.1 = (bf16[1536,2,128]{2,1,0:T(2,128)(2,1)S(1)}, bf16[1536,2,128]{2,1,0:T(2,128)(2,1)S(1)}, u32[]{:S(2)}, u32[]{:S(2)}) collective-permute-start(bf16[1536,2,128]{2,1,0:T(2,128)(2,1)S(1)} %bitcast.34), channel_id=1, source_target_pairs={{0,64},{64,0},{1,65},{65,1},{2,66},{66,2},{3,67},{67,3},{4,68},{68... | collective-permute-start | bytes 2359304 | tf_op jit(solution)/shard_map/ppermute | solution.py:404

commit v6 on v5

--- a/solution.py
+++ b/solution.py
@@ -18,7 +18,7 @@
 WAVE = 0.0197
 AMP = 0.1
 VMEM_LIMIT = 40 * 1024 * 1024
-FINE = ("zh", "c", "y", "x", "zl")
+FINE = ("zh", "c", "yh", "yl", "x", "zl")
 F32 = jnp.float32
 BF16 = jnp.bfloat16
 
@@ -79,7 +79,7 @@
     y = lax.shift_right_logical(own, 3) & 7
     x = lax.shift_right_logical(own, 1) & 3
     across = ((lax.shift_right_logical(own, 6) ^ lax.shift_right_logical(me, 6)) & 1) * HALF
-    pos_ref[...] = 2 * (across + (x * 2 + (own & 1)) * (32 * CAP) + (z * 8 + y) * CAP + jnp.minimum(slots, CAP - 1))
+    pos_ref[...] = 2 * (across + (x * 4 + (own & 1) * 2 + (y & 1)) * (16 * CAP) + (z * 4 + lax.shift_right_logical(y, 1)) * CAP + jnp.minimum(slots, CAP - 1))
     parity = (iota((8, 128), 0) & 1) == 0
     row_pair = lax.shift_right_logical(iota((1024, 128), 0), 1)
     lo_iota = iota((128, 128), 0)
@@ -101,7 +101,7 @@
             stage[copy * 12 + 2 * k : copy * 12 + 2 * k + 1, :] = re
             stage[copy * 12 + 2 * k + 1 : copy * 12 + 2 * k + 2, :] = im
     block = stage[...].astype(BF16)
-    for copy in range(4):
+    for copy in range(2):
         out_ref[copy * 96 : (copy + 1) * 96, :] = block
 
 
@@ -244,7 +244,7 @@
 def insert_kernel(mine_ref, got_ref, out_hbm, wide, left, right, out, sems):
     hi_iota = iota((512, 128), 0)
     lo_iota = iota((128, 128), 0)
-    sums = jnp.sum(got_ref[...].astype(F32).reshape(16, 24, 128), axis=0)
+    sums = jnp.sum(got_ref[...].astype(F32).reshape(8, 24, 128), axis=0)
     wide[...] = sums * (1.0 / math.sqrt(PARTICLES))
     for k in range(CAP):
         vox = mine_ref[k : k + 1, :]
@@ -278,9 +278,9 @@
 
 
 def line_kernel(got_ref, out_ref):
-    total = got_ref[0:384, :].astype(F32)
-    for k in range(1, 8):
-        total = total + got_ref[k * 384 : (k + 1) * 384, :].astype(F32)
+    total = got_ref[0:192, :].astype(F32)
+    for k in range(1, 16):
+        total = total + got_ref[k * 192 : (k + 1) * 192, :].astype(F32)
     out_ref[...] = total.astype(BF16)
 
 
@@ -307,7 +307,7 @@
         out_shape=(
             shape((REFS, KY), jnp.int32),
             shape((8, 128), jnp.int32),
-            shape((32 * 12, 128), BF16),
+            shape((16 * 12, 128), BF16),
         ),
         in_specs=[SM, ANY, ANY, ANY],
         out_specs=(VM, VM, VM),
@@ -319,7 +319,7 @@
             pltpu.VMEM((ROWS, KX), jnp.int32),
             pltpu.SemaphoreType.DMA((3,)),
         ],
-        compiler_params=pltpu.CompilerParams(vmem_limit_bytes=107 * 512 * 1024),
+        compiler_params=pltpu.CompilerParams(vmem_limit_bytes=430 * 128 * 1024),
         name="pick_rows",
     )(me, owner, volume_rows, voxel_rows)
 
@@ -392,9 +392,9 @@
     me = lax.axis_index(FINE).astype(jnp.int32).reshape(1)
     volume_rows = volume.reshape(2, 512, 128).transpose(1, 0, 2).reshape(1024, 128)
     pos, mine, compact = pick_call(me, slice_owner, volume_rows, slice_voxel.reshape(ROWS, KX))
-    line = lax.all_to_all(compact.reshape(32, CAP, 2, 128), ("zh", "y"), 0, 0, tiled=True)
-    spread = jnp.broadcast_to(line.reshape(1, 192, 2, 128), (8, 192, 2, 128))
-    near = lax.all_to_all(spread, ("x", "zl"), 0, 0, tiled=True).reshape(HALF, 2, 128)
+    line = lax.all_to_all(compact.reshape(16, CAP, 2, 128), ("zh", "yh"), 0, 0, tiled=True)
+    spread = jnp.broadcast_to(line.reshape(1, 96, 2, 128), (16, 96, 2, 128))
+    near = lax.all_to_all(spread, ("x", "zl", "yl"), 0, 0, tiled=True).reshape(HALF, 2, 128)
     swap = [(0, 1), (1, 0)]
     far = lax.ppermute(near, "c", swap)
     img, sq = image_call(defocus, particles.reshape(PER * KY * 2, KX))
@@ -403,14 +403,14 @@
     )
     received = lax.ppermute(far_out.reshape(HALF, 2, 128), "c", swap)
     pair = small_call(pair_kernel, "add_core", 2 * HALF, sums, received.reshape(2 * HALF, 128))
-    plane = lax.all_to_all(pair.reshape(8, 192, 2, 128), ("x", "zl"), 0, 0, tiled=True)
-    plane = small_call(line_kernel, "add_line", 384, plane.reshape(2 * HALF, 128))
-    last = lax.all_to_all(plane.reshape(32, CAP, 2, 128), ("zh", "y"), 0, 0, tiled=True)
-    out = insert_call(mine, last.reshape(384, 128))
+    plane = lax.all_to_all(pair.reshape(16, 96, 2, 128), ("x", "zl", "yl"), 0, 0, tiled=True)
+    plane = small_call(line_kernel, "add_line", 192, plane.reshape(2 * HALF, 128))
+    last = lax.all_to_all(plane.reshape(16, CAP, 2, 128), ("zh", "yh"), 0, 0, tiled=True)
+    out = insert_call(mine, last.reshape(192, 128))
     return out.reshape(512, 2, 128).transpose(1, 0, 2).reshape(2, 65536)
 
 
 def solution(mesh):
-    fine = Mesh(mesh.devices.reshape(4, 2, 8, 4, 2), FINE)
+    fine = Mesh(mesh.devices.reshape(4, 2, 4, 2, 4, 2), FINE)
     in_specs = (P(FINE, None, None, None), P(FINE), P(FINE), P(None, FINE), P(), P())
     return jax.shard_map(local, mesh=fine, in_specs=in_specs, out_specs=P(None, FINE), check_vma=False)

time: 101 us -> 101 us (level)
  no operation moved by 1% of the time
where the time goes in v6:
time: 101 us; the launch traced here: 100 us
  blocking collectives  76 us (75%)
  Pallas kernels  16 us (16%)
  starting transfers between devices  3.95 us (4%)
  waiting for transfers between devices  2.93 us (3%)
  local copies, waits for them, and re-layouts  1.35 us (1%)
    all_to_all x1, blocking collectives, local(): lax.all_to_all(compact.reshape(16, CAP, 2, 128), ('zh', 'yh'), 0, 0, tile...  27 us
    all_to_all x1, blocking collectives, local(): lax.all_to_all(spread, ('x', 'zl', 'yl'), 0, 0, tiled=True)  17.2 us
    all_to_all x1, blocking collectives, local(): lax.all_to_all(pair.reshape(16, 96, 2, 128), ('x', 'zl', 'yl'), 0, 0, til...  16.8 us
    all_to_all x1, blocking collectives, local(): lax.all_to_all(plane.reshape(16, CAP, 2, 128), ('zh', 'yh'), 0, 0, tiled=...  15 us
    pallas_call x1, Pallas kernels, search_call(): pl.pallas_call(search_kernel, out_shape=(shape((4 * HALF, KX), F32), shap...  10.9 us
    ppermute x1, waiting for transfers between devices, local(): received = lax.ppermute(far_out.reshape(HALF, 2, 128), 'c', swap)  2.13 us
    ppermute x1, starting transfers between devices, local(): received = lax.ppermute(far_out.reshape(HALF, 2, 128), 'c', swap)  2.04 us
  transfers between devices with their start and end apart: 2, of which 2 were waited for; matrix products, arithmetic and copies ran while one was open for 0% of the time, Pallas kernels for 1%

profile of v6, /device:TPU:8, one launch (start us, length us, event | category | flops | bytes accessed | tf_op | source)
XLA Modules:
  0.0 100.4 jit_solution(10327580214660987853)
XLA Ops:
  0.0 0.0 copy-start.7
  0.0 0.0 copy-start.4
  0.0 0.7 copy-done.4
  0.7 0.0 copy-start.6
  0.7 2.0 %pick_rows.1 = (s32[8,256]{1,0:T(8,128)S(1)}, s32[8,128]{1,0:T(8,128)S(1)}, bf16[192,128]{1,0:T(8,128)(2,1)S(1)}) custom-call(s32[1]{0:T(128)} %bitcast.me_ref, s32[8,256]{1,0:T(8,128)S(1)} %copy-done.4, bf16[1024,128]{1,0:T(8,128)(2,1)} %bitcast.36, s32[2048,128]{1,0:T(8,128)} %bitcast.35), custom_call_target="tpu_custom_call" | custom-call | tf_op jit(solution)/shard_map/pick_rows/pallas_call | solution.py:305
  2.7 27.0 %all_to_all.20 = bf16[16,6,2,128]{3,2,1,0:T(2,128)(2,1)S(1)} all-to-all(bf16[16,6,2,128]{3,2,1,0:T(2,128)(2,1)S(1)} %bitcast.32), channel_id=1, replica_groups=mesh['zh'=4,'c'=2,'yh'=4,'yl'=2,'x'=4,'zl'=2] {'zh','yh'}, dimensions={0} | all-to-all | bytes 98304 | tf_op jit(solution)/shard_map/all_to_all | solution.py:395
  29.7 0.6 broadcast_in_dim.8
  30.3 17.2 %all_to_all.21 = bf16[16,96,2,128]{3,2,1,0:T(2,128)(2,1)S(1)} all-to-all(bf16[16,96,2,128]{3,2,1,0:T(2,128)(2,1)S(1)} %broadcast_in_dim.8), channel_id=1, replica_groups=mesh['zh'=4,'c'=2,'yh'=4,'yl'=2,'x'=4,'zl'=2] {'x','zl','yl'}, dimensions={0} | all-to-all | bytes 1572864 | tf_op jit(solution)/shard_map/all_to_all | solution.py:397
  47.5 1.9 %collective-permute-start = (bf16[1536,2,128]{2,1,0:T(2,128)(2,1)S(1)}, bf16[1536,2,128]{2,1,0:T(2,128)(2,1)S(1)}, u32[]{:S(2)}, u32[]{:S(2)}) collective-permute-start(bf16[1536,2,128]{2,1,0:T(2,128)(2,1)S(1)} %bitcast.24), channel_id=1, source_target_pairs={{0,64},{64,0},{1,65},{65,1},{2,66},{66,2},{3,67},{67,3},{4,68},{68... | collective-permute-start | bytes 2359304 | tf_op jit(solution)/shard_map/ppermute | solution.py:399
  49.4 0.0 copy-done.7
  49.4 0.0 copy-done.6
  49.5 0.0 copy-start
  49.5 0.0 copy-start.1
  49.5 0.0 copy-start.2
  49.5 0.0 copy-start.3
  49.5 0.0 copy-start.5
  49.5 1.4 %ctf_images.1 = (f32[2048,128]{1,0:T(8,128)S(1)}, f32[1024,128]{1,0:T(8,128)S(1)}) custom-call(f32[4]{0:T(128)S(1)} %copy-done.7, bf16[2048,128]{1,0:T(8,128)(2,1)S(1)} %bitcast.34), custom_call_target="tpu_custom_call" | custom-call | flops 4000000000 | bytes 4000000 | tf_op jit(solution)/shard_map/ctf_images/pallas_call | solution.py:328
  50.9 0.8 collective-permute-done
  51.7 0.0 copy-done
  51.7 0.0 copy-done.1
  51.7 0.0 copy-done.2
  51.7 0.0 copy-done.3
  51.7 0.0 copy-done.5
  51.7 10.9 %shift_search.1 = (f32[6144,128]{1,0:T(8,128)S(1)}, bf16[3072,128]{1,0:T(8,128)(2,1)S(1)}) custom-call(s32[8,256]{1,0:T(8,128)S(1)} %get-tuple-element.13.pos_ref, f32[4]{0:T(128)S(1)} %copy-done.5, bf16[3072,128]{1,0:T(8,128)(2,1)S(1)} %bitcast.25, bf16[3072,128]{1,0:T(8,128)(2,1)S(1)} %bitcast.28, f32[2048,128]{1,0:T(8,128)S(1)} %get-tuple-element.15.img_ref, ...), custom_call_target="tpu_custom_call" | custom-call | tf_op jit(solution)/shard_map/shift_search/pallas_call | solution.py:342
  62.7 2.0 %collective-permute-start.1 = (bf16[1536,2,128]{2,1,0:T(2,128)(2,1)S(1)}, bf16[1536,2,128]{2,1,0:T(2,128)(2,1)S(1)}, u32[]{:S(2)}, u32[]{:S(2)}) collective-permute-start(bf16[1536,2,128]{2,1,0:T(2,128)(2,1)S(1)} %bitcast.33), channel_id=1, source_target_pairs={{0,64},{64,0},{1,65},{65,1},{2,66},{66,2},{3,67},{67,3},{4,68},{68... | collective-permute-start | bytes 2359304 | tf_op jit(solution)/shard_map/ppermute | solution.py:404
  64.7 2.1 %collective-permute-done.1 = bf16[1536,2,128]{2,1,0:T(2,128)(2,1)S(1)} collective-permute-done((bf16[1536,2,128]{2,1,0:T(2,128)(2,1)S(1)}, bf16[1536,2,128]{2,1,0:T(2,128)(2,1)S(1)}, u32[]{:S(2)}, u32[]{:S(2)}) %collective-permute-start.1) | collective-permute-done | bytes 786464 | tf_op jit(solution)/shard_map/ppermute | solution.py:404
  66.8 0.2 add_core.1
  67.1 16.8 %all_to_all.22 = bf16[16,96,2,128]{3,2,1,0:T(2,128)(2,1)S(1)} all-to-all(bf16[16,96,2,128]{3,2,1,0:T(2,128)(2,1)S(1)} %bitcast.26), channel_id=1, replica_groups=mesh['zh'=4,'c'=2,'yh'=4,'yl'=2,'x'=4,'zl'=2] {'x','zl','yl'}, dimensions={0} | all-to-all | bytes 1572864 | tf_op jit(solution)/shard_map/all_to_all | solution.py:406
  83.9 0.1 add_line.1
  84.0 15.0 %all_to_all.23 = bf16[16,6,2,128]{3,2,1,0:T(2,128)(2,1)S(1)} all-to-all(bf16[16,6,2,128]{3,2,1,0:T(2,128)(2,1)S(1)} %bitcast.31), channel_id=1, replica_groups=mesh['zh'=4,'c'=2,'yh'=4,'yl'=2,'x'=4,'zl'=2] {'zh','yh'}, dimensions={0} | all-to-all | bytes 98304 | tf_op jit(solution)/shard_map/all_to_all | solution.py:408
  99.0 1.4 %insert_rows.1 = f32[1024,128]{1,0:T(8,128)} custom-call(s32[8,128]{1,0:T(8,128)S(1)} %get-tuple-element.12.mine_ref, bf16[192,128]{1,0:T(8,128)(2,1)S(1)} %bitcast.30), custom_call_target="tpu_custom_call" | custom-call | tf_op jit(solution)/shard_map/insert_rows/pallas_call | solution.py:374
Async XLA Ops:
  0.0 49.4 %copy-start.7 = (f32[4]{0:T(128)S(1)}, f32[4]{0:T(128)}, u32[]{:S(2)}) copy-start(f32[4]{0:T(128)} %defocus_ref.1) | copy-start | bytes 52
  0.0 0.7 copy-start.4
  0.7 48.7 %copy-start.6 = (bf16[4,256,2,128]{3,2,1,0:T(2,128)(2,1)S(1)}, bf16[4,256,2,128]{3,2,1,0:T(2,128)(2,1)}, u32[]{:S(2)}) copy-start(bf16[4,256,2,128]{3,2,1,0:T(2,128)(2,1)} %param.10) | copy-start | bytes 1572868
  47.5 4.2 %collective-permute-start = (bf16[1536,2,128]{2,1,0:T(2,128)(2,1)S(1)}, bf16[1536,2,128]{2,1,0:T(2,128)(2,1)S(1)}, u32[]{:S(2)}, u32[]{:S(2)}) collective-permute-start(bf16[1536,2,128]{2,1,0:T(2,128)(2,1)S(1)} %bitcast.24), channel_id=1, source_target_pairs={{0,64},{64,0},{1,65},{65,1},{2,66},{66,2},{3,67},{67,3},{4,68},{68... | collective-permute-start | bytes 2359304 | tf_op jit(solution)/shard_map/ppermute | solution.py:399
  49.5 2.2 %copy-start = (bf16[256,1024]{1,0:T(8,128)(2,1)S(1)}, bf16[256,1024]{1,0:T(8,128)(2,1)}, u32[]{:S(2)}) copy-start(bf16[256,1024]{1,0:T(8,128)(2,1)} %constant.42.clone.bwd_ref) | copy-start | bytes 1572868
  49.5 2.2 %copy-start.1 = (bf16[1024,256]{1,0:T(8,128)(2,1)S(1)}, bf16[1024,256]{1,0:T(8,128)(2,1)}, u32[]{:S(2)}) copy-start(bf16[1024,256]{1,0:T(8,128)(2,1)} %constant.41.clone.fwd_ref) | copy-start | bytes 1572868
  49.5 2.2 %copy-start.2 = (bf16[512,32]{1,0:T(8,128)(2,1)S(1)}, bf16[512,32]{1,0:T(8,128)(2,1)}, u32[]{:S(2)}) copy-start(bf16[512,32]{1,0:T(8,128)(2,1)} %constant.44.clone.back_ref) | copy-start | bytes 98308
  49.5 2.2 %copy-start.3 = (bf16[64,256]{1,0:T(8,128)(2,1)S(1)}, bf16[64,256]{1,0:T(8,128)(2,1)}, u32[]{:S(2)}) copy-start(bf16[64,256]{1,0:T(8,128)(2,1)} %constant.43.clone.corr_ref) | copy-start | bytes 98308
  49.5 2.2 %copy-start.5 = (f32[4]{0:T(128)S(1)}, f32[4]{0:T(128)}, u32[]{:S(2)}) copy-start(f32[4]{0:T(128)} %noise_ref.1) | copy-start | bytes 52
  62.7 4.2 %collective-permute-start.1 = (bf16[1536,2,128]{2,1,0:T(2,128)(2,1)S(1)}, bf16[1536,2,128]{2,1,0:T(2,128)(2,1)S(1)}, u32[]{:S(2)}, u32[]{:S(2)}) collective-permute-start(bf16[1536,2,128]{2,1,0:T(2,128)(2,1)S(1)} %bitcast.33), channel_id=1, source_target_pairs={{0,64},{64,0},{1,65},{65,1},{2,66},{66,2},{3,67},{67,3},{4,68},{68... | collective-permute-start | bytes 2359304 | tf_op jit(solution)/shard_map/ppermute | solution.py:404

commit v7 on v6

--- a/solution.py
+++ b/solution.py
@@ -132,7 +132,12 @@
 
 
 CH = 64
-BIG = 1024
+
+
+def mul(at, size):
+    return at if isinstance(at, int) else pl.multiple_of(at, size)
+
+
 PIECES = 2
 
 
@@ -164,8 +169,8 @@
             mag = re * re + im * im
             for p in range(PER):
                 a_re, a_im = images(p, k)
-                q[pl.ds(pl.multiple_of(r * KY + k * CH, CH), CH), p * 256 : p * 256 + 128] = (re * a_re + im * a_im).astype(BF16)
-                q[pl.ds(pl.multiple_of(r * KY + k * CH, CH), CH), p * 256 + 128 : (p + 1) * 256] = (re * a_im - im * a_re).astype(BF16)
+                q[pl.ds(mul(r * KY + k * CH, CH), CH), p * 256 : p * 256 + 128] = (re * a_re + im * a_im).astype(BF16)
+                q[pl.ds(mul(r * KY + k * CH, CH), CH), p * 256 + 128 : (p + 1) * 256] = (re * a_im - im * a_re).astype(BF16)
                 part = sq_ref[p * KY + k * CH : p * KY + (k + 1) * CH, :] * mag
                 sums[p] = sums[p] + jnp.sum(part.reshape(CH // 8, 8, KX), axis=0)
         for p in range(PER):
@@ -179,10 +184,17 @@
 
     for k in range(KY // CH):
         fetch(0, rows_a, k)
-    lax.fori_loop(0, REFS // 2, forward, 0)
-    for m in range(ROWS // BIG):
-        at = slice(m * BIG, (m + 1) * BIG)
+    def turn(start, size):
+        at = slice(start, start + size)
         row_phase[at, :] = jnp.dot(q[at, :], fwd_ref[...], preferred_element_type=F32).astype(BF16)
+
+    lax.fori_loop(0, REFS // 4, forward, 0)
+    half = REFS // 2
+    for r in range(half, REFS):
+        buffers = (rows_a, rows_b) if r % 2 == 0 else (rows_b, rows_a)
+        turn((r - half) * KY, KY)
+        score_ref(r, buffers[0], min(r + 1, REFS - 1), buffers[1])
+    turn(half * KY, half * KY)
     for r in range(REFS):
         both = jnp.dot(corr_ref[...], row_phase[r * KY : (r + 1) * KY, :], preferred_element_type=F32)
         corr[r * SHIFTS : (r + 1) * SHIFTS, :] = both[:SHIFTS, :128] - both[SHIFTS:, 128:]
@@ -210,7 +222,7 @@
     sum_ref[...] = jnp.zeros_like(sum_ref)
 
     def insert_ref(r, rows, behind, behind_rows):
-        w = weight[pl.ds(pl.multiple_of(r * SHIFTS, SHIFTS), SHIFTS), :]
+        w = weight[pl.ds(mul(r * SHIFTS, SHIFTS), SHIFTS), :]
         col = jnp.dot(back_ref[...], w, preferred_element_type=F32).astype(BF16)
         col = jnp.concatenate([col[:KY], col[KY:]], axis=1)
         shifted = jnp.dot(col, bwd_ref[...], preferred_element_type=F32).astype(BF16)

time: 101 us -> 100 us (0.990)
  no operation moved by 1% of the time
where the time goes in v7:
time: 100 us; the launch traced here: 99.9 us
  blocking collectives  76 us (76%)
  Pallas kernels  15.5 us (16%)
  starting transfers between devices  3.95 us (4%)
  waiting for transfers between devices  2.93 us (3%)
  local copies, waits for them, and re-layouts  1.35 us (1%)
    all_to_all x1, blocking collectives, local(): lax.all_to_all(compact.reshape(16, CAP, 2, 128), ('zh', 'yh'), 0, 0, tile...  27 us
    all_to_all x1, blocking collectives, local(): lax.all_to_all(spread, ('x', 'zl', 'yl'), 0, 0, tiled=True)  17.2 us
    all_to_all x1, blocking collectives, local(): lax.all_to_all(pair.reshape(16, 96, 2, 128), ('x', 'zl', 'yl'), 0, 0, til...  16.8 us
    all_to_all x1, blocking collectives, local(): lax.all_to_all(plane.reshape(16, CAP, 2, 128), ('zh', 'yh'), 0, 0, tiled=...  15 us
    pallas_call x1, Pallas kernels, search_call(): pl.pallas_call(search_kernel, out_shape=(shape((4 * HALF, KX), F32), shap...  10.4 us
    ppermute x1, waiting for transfers between devices, local(): received = lax.ppermute(far_out.reshape(HALF, 2, 128), 'c', swap)  2.13 us
    ppermute x1, starting transfers between devices, local(): received = lax.ppermute(far_out.reshape(HALF, 2, 128), 'c', swap)  2.04 us
  transfers between devices with their start and end apart: 2, of which 2 were waited for; matrix products, arithmetic and copies ran while one was open for 0% of the time, Pallas kernels for 1%

profile of v7, /device:TPU:8, one launch (start us, length us, event | category | flops | bytes accessed | tf_op | source)
XLA Modules:
  0.0 99.9 jit_solution(10510705661010394472)
XLA Ops:
  0.0 0.0 copy-start.7
  0.0 0.0 copy-start.4
  0.0 0.7 copy-done.4
  0.7 0.0 copy-start.6
  0.7 2.0 %pick_rows.1 = (s32[8,256]{1,0:T(8,128)S(1)}, s32[8,128]{1,0:T(8,128)S(1)}, bf16[192,128]{1,0:T(8,128)(2,1)S(1)}) custom-call(s32[1]{0:T(128)} %bitcast.me_ref, s32[8,256]{1,0:T(8,128)S(1)} %copy-done.4, bf16[1024,128]{1,0:T(8,128)(2,1)} %bitcast.36, s32[2048,128]{1,0:T(8,128)} %bitcast.35), custom_call_target="tpu_custom_call" | custom-call | tf_op jit(solution)/shard_map/pick_rows/pallas_call | solution.py:317
  2.7 27.0 %all_to_all.20 = bf16[16,6,2,128]{3,2,1,0:T(2,128)(2,1)S(1)} all-to-all(bf16[16,6,2,128]{3,2,1,0:T(2,128)(2,1)S(1)} %bitcast.32), channel_id=1, replica_groups=mesh['zh'=4,'c'=2,'yh'=4,'yl'=2,'x'=4,'zl'=2] {'zh','yh'}, dimensions={0} | all-to-all | bytes 98304 | tf_op jit(solution)/shard_map/all_to_all | solution.py:407
  29.7 0.6 broadcast_in_dim.8
  30.3 17.2 %all_to_all.21 = bf16[16,96,2,128]{3,2,1,0:T(2,128)(2,1)S(1)} all-to-all(bf16[16,96,2,128]{3,2,1,0:T(2,128)(2,1)S(1)} %broadcast_in_dim.8), channel_id=1, replica_groups=mesh['zh'=4,'c'=2,'yh'=4,'yl'=2,'x'=4,'zl'=2] {'x','zl','yl'}, dimensions={0} | all-to-all | bytes 1572864 | tf_op jit(solution)/shard_map/all_to_all | solution.py:409
  47.5 1.9 %collective-permute-start = (bf16[1536,2,128]{2,1,0:T(2,128)(2,1)S(1)}, bf16[1536,2,128]{2,1,0:T(2,128)(2,1)S(1)}, u32[]{:S(2)}, u32[]{:S(2)}) collective-permute-start(bf16[1536,2,128]{2,1,0:T(2,128)(2,1)S(1)} %bitcast.24), channel_id=1, source_target_pairs={{0,64},{64,0},{1,65},{65,1},{2,66},{66,2},{3,67},{67,3},{4,68},{68... | collective-permute-start | bytes 2359304 | tf_op jit(solution)/shard_map/ppermute | solution.py:411
  49.4 0.0 copy-done.7
  49.4 0.0 copy-done.6
  49.5 0.0 copy-start
  49.5 0.0 copy-start.1
  49.5 0.0 copy-start.2
  49.5 0.0 copy-start.3
  49.5 0.0 copy-start.5
  49.5 1.4 %ctf_images.1 = (f32[2048,128]{1,0:T(8,128)S(1)}, f32[1024,128]{1,0:T(8,128)S(1)}) custom-call(f32[4]{0:T(128)S(1)} %copy-done.7, bf16[2048,128]{1,0:T(8,128)(2,1)S(1)} %bitcast.34), custom_call_target="tpu_custom_call" | custom-call | flops 4000000000 | bytes 4000000 | tf_op jit(solution)/shard_map/ctf_images/pallas_call | solution.py:340
  50.9 0.8 collective-permute-done
  51.7 0.0 copy-done
  51.7 0.0 copy-done.1
  51.7 0.0 copy-done.2
  51.7 0.0 copy-done.3
  51.7 0.0 copy-done.5
  51.7 10.4 %shift_search.1 = (f32[6144,128]{1,0:T(8,128)S(1)}, bf16[3072,128]{1,0:T(8,128)(2,1)S(1)}) custom-call(s32[8,256]{1,0:T(8,128)S(1)} %get-tuple-element.13.pos_ref, f32[4]{0:T(128)S(1)} %copy-done.5, bf16[3072,128]{1,0:T(8,128)(2,1)S(1)} %bitcast.25, bf16[3072,128]{1,0:T(8,128)(2,1)S(1)} %bitcast.28, f32[2048,128]{1,0:T(8,128)S(1)} %get-tuple-element.15.img_ref, ...), custom_call_target="tpu_custom_call" | custom-call | tf_op jit(solution)/shard_map/shift_search/pallas_call | solution.py:354
  62.2 2.0 %collective-permute-start.1 = (bf16[1536,2,128]{2,1,0:T(2,128)(2,1)S(1)}, bf16[1536,2,128]{2,1,0:T(2,128)(2,1)S(1)}, u32[]{:S(2)}, u32[]{:S(2)}) collective-permute-start(bf16[1536,2,128]{2,1,0:T(2,128)(2,1)S(1)} %bitcast.33), channel_id=1, source_target_pairs={{0,64},{64,0},{1,65},{65,1},{2,66},{66,2},{3,67},{67,3},{4,68},{68... | collective-permute-start | bytes 2359304 | tf_op jit(solution)/shard_map/ppermute | solution.py:416
  64.2 2.1 %collective-permute-done.1 = bf16[1536,2,128]{2,1,0:T(2,128)(2,1)S(1)} collective-permute-done((bf16[1536,2,128]{2,1,0:T(2,128)(2,1)S(1)}, bf16[1536,2,128]{2,1,0:T(2,128)(2,1)S(1)}, u32[]{:S(2)}, u32[]{:S(2)}) %collective-permute-start.1) | collective-permute-done | bytes 786464 | tf_op jit(solution)/shard_map/ppermute | solution.py:416
  66.3 0.2 add_core.1
  66.6 16.8 %all_to_all.22 = bf16[16,96,2,128]{3,2,1,0:T(2,128)(2,1)S(1)} all-to-all(bf16[16,96,2,128]{3,2,1,0:T(2,128)(2,1)S(1)} %bitcast.26), channel_id=1, replica_groups=mesh['zh'=4,'c'=2,'yh'=4,'yl'=2,'x'=4,'zl'=2] {'x','zl','yl'}, dimensions={0} | all-to-all | bytes 1572864 | tf_op jit(solution)/shard_map/all_to_all | solution.py:418
  83.4 0.1 add_line.1
  83.5 15.0 %all_to_all.23 = bf16[16,6,2,128]{3,2,1,0:T(2,128)(2,1)S(1)} all-to-all(bf16[16,6,2,128]{3,2,1,0:T(2,128)(2,1)S(1)} %bitcast.31), channel_id=1, replica_groups=mesh['zh'=4,'c'=2,'yh'=4,'yl'=2,'x'=4,'zl'=2] {'zh','yh'}, dimensions={0} | all-to-all | bytes 98304 | tf_op jit(solution)/shard_map/all_to_all | solution.py:420
  98.5 1.4 %insert_rows.1 = f32[1024,128]{1,0:T(8,128)} custom-call(s32[8,128]{1,0:T(8,128)S(1)} %get-tuple-element.12.mine_ref, bf16[192,128]{1,0:T(8,128)(2,1)S(1)} %bitcast.30), custom_call_target="tpu_custom_call" | custom-call | tf_op jit(solution)/shard_map/insert_rows/pallas_call | solution.py:386
Async XLA Ops:
  0.0 49.4 %copy-start.7 = (f32[4]{0:T(128)S(1)}, f32[4]{0:T(128)}, u32[]{:S(2)}) copy-start(f32[4]{0:T(128)} %defocus_ref.1) | copy-start | bytes 52
  0.0 0.7 copy-start.4
  0.7 48.7 %copy-start.6 = (bf16[4,256,2,128]{3,2,1,0:T(2,128)(2,1)S(1)}, bf16[4,256,2,128]{3,2,1,0:T(2,128)(2,1)}, u32[]{:S(2)}) copy-start(bf16[4,256,2,128]{3,2,1,0:T(2,128)(2,1)} %param.10) | copy-start | bytes 1572868
  47.5 4.2 %collective-permute-start = (bf16[1536,2,128]{2,1,0:T(2,128)(2,1)S(1)}, bf16[1536,2,128]{2,1,0:T(2,128)(2,1)S(1)}, u32[]{:S(2)}, u32[]{:S(2)}) collective-permute-start(bf16[1536,2,128]{2,1,0:T(2,128)(2,1)S(1)} %bitcast.24), channel_id=1, source_target_pairs={{0,64},{64,0},{1,65},{65,1},{2,66},{66,2},{3,67},{67,3},{4,68},{68... | collective-permute-start | bytes 2359304 | tf_op jit(solution)/shard_map/ppermute | solution.py:411
  49.5 2.2 %copy-start = (bf16[256,1024]{1,0:T(8,128)(2,1)S(1)}, bf16[256,1024]{1,0:T(8,128)(2,1)}, u32[]{:S(2)}) copy-start(bf16[256,1024]{1,0:T(8,128)(2,1)} %constant.42.clone.bwd_ref) | copy-start | bytes 1572868
  49.5 2.2 %copy-start.1 = (bf16[1024,256]{1,0:T(8,128)(2,1)S(1)}, bf16[1024,256]{1,0:T(8,128)(2,1)}, u32[]{:S(2)}) copy-start(bf16[1024,256]{1,0:T(8,128)(2,1)} %constant.41.clone.fwd_ref) | copy-start | bytes 1572868
  49.5 2.2 %copy-start.2 = (bf16[512,32]{1,0:T(8,128)(2,1)S(1)}, bf16[512,32]{1,0:T(8,128)(2,1)}, u32[]{:S(2)}) copy-start(bf16[512,32]{1,0:T(8,128)(2,1)} %constant.44.clone.back_ref) | copy-start | bytes 98308
  49.5 2.2 %copy-start.3 = (bf16[64,256]{1,0:T(8,128)(2,1)S(1)}, bf16[64,256]{1,0:T(8,128)(2,1)}, u32[]{:S(2)}) copy-start(bf16[64,256]{1,0:T(8,128)(2,1)} %constant.43.clone.corr_ref) | copy-start | bytes 98308
  49.5 2.2 %copy-start.5 = (f32[4]{0:T(128)S(1)}, f32[4]{0:T(128)}, u32[]{:S(2)}) copy-start(f32[4]{0:T(128)} %noise_ref.1) | copy-start | bytes 52
  62.2 4.2 %collective-permute-start.1 = (bf16[1536,2,128]{2,1,0:T(2,128)(2,1)S(1)}, bf16[1536,2,128]{2,1,0:T(2,128)(2,1)S(1)}, u32[]{:S(2)}, u32[]{:S(2)}) collective-permute-start(bf16[1536,2,128]{2,1,0:T(2,128)(2,1)S(1)} %bitcast.33), channel_id=1, source_target_pairs={{0,64},{64,0},{1,65},{65,1},{2,66},{66,2},{3,67},{67,3},{4,68},{68... | collective-permute-start | bytes 2359304 | tf_op jit(solution)/shard_map/ppermute | solution.py:416

commit v8 on v7

--- a/solution.py
+++ b/solution.py
@@ -48,16 +48,13 @@
     return lax.broadcasted_iota(jnp.int32, shape, dim)
 
 
-def pick_kernel(me_ref, own_hbm, vol_hbm, vox_hbm, pos_ref, mine_ref, out_ref, owners, slot, stage, table, voxels, sems):
-    load_own = pltpu.make_async_copy(own_hbm, owners, sems.at[0])
-    load_vox = pltpu.make_async_copy(vox_hbm, voxels, sems.at[1])
-    load_vol = pltpu.make_async_copy(vol_hbm, table, sems.at[2])
-    load_own.start()
+def pick_kernel(me_ref, own_ref, vol_hbm, vox_hbm, pos_ref, mine_ref, out_ref, slot, stage, table, voxels, sems):
+    load_vox = pltpu.make_async_copy(vox_hbm, voxels, sems.at[0])
+    load_vol = pltpu.make_async_copy(vol_hbm, table, sems.at[1])
     load_vox.start()
     load_vol.start()
     me = me_ref[0]
-    load_own.wait()
-    own = owners[...]
+    own = own_ref[...]
     turned = own.astype(F32).T
     cols, here = [], []
     for b in range(ROWS // 128):
@@ -321,15 +318,14 @@
             shape((8, 128), jnp.int32),
             shape((16 * 12, 128), BF16),
         ),
-        in_specs=[SM, ANY, ANY, ANY],
+        in_specs=[SM, VM, ANY, ANY],
         out_specs=(VM, VM, VM),
         scratch_shapes=[
-            pltpu.VMEM((REFS, KY), jnp.int32),
             pltpu.VMEM((REFS, KY), jnp.int32),
             pltpu.VMEM((96, 128), F32),
             pltpu.VMEM((1024, 128), BF16),
             pltpu.VMEM((ROWS, KX), jnp.int32),
-            pltpu.SemaphoreType.DMA((3,)),
+            pltpu.SemaphoreType.DMA((2,)),
         ],
         compiler_params=pltpu.CompilerParams(vmem_limit_bytes=430 * 128 * 1024),
         name="pick_rows",

time: 100 us -> 101 us (1.010)
    pallas_call x1, Pallas kernels: 1.96 us -> 2.99 us  [pick_call(): pl.pallas_call(pick_kernel, out_shape=(shape((REFS, KY), jnp.int32), shap...]
where the time goes in v8:
time: 101 us
  blocking collectives  76 us (75%)
  Pallas kernels  16.5 us (16%)
  starting transfers between devices  3.94 us (4%)
  waiting for transfers between devices  2.94 us (3%)
  local copies, waits for them, and re-layouts  1.35 us (1%)
    all_to_all x1, blocking collectives, local(): lax.all_to_all(compact.reshape(16, CAP, 2, 128), ('zh', 'yh'), 0, 0, tile...  27 us
    all_to_all x1, blocking collectives, local(): lax.all_to_all(spread, ('x', 'zl', 'yl'), 0, 0, tiled=True)  17.2 us
    all_to_all x1, blocking collectives, local(): lax.all_to_all(pair.reshape(16, 96, 2, 128), ('x', 'zl', 'yl'), 0, 0, til...  16.8 us
    all_to_all x1, blocking collectives, local(): lax.all_to_all(plane.reshape(16, CAP, 2, 128), ('zh', 'yh'), 0, 0, tiled=...  15 us
    pallas_call x1, Pallas kernels, search_call(): pl.pallas_call(search_kernel, out_shape=(shape((4 * HALF, KX), F32), shap...  10.4 us
    pallas_call x1, Pallas kernels, pick_call(): pl.pallas_call(pick_kernel, out_shape=(shape((REFS, KY), jnp.int32), shap...  2.99 us
    ppermute x1, waiting for transfers between devices, local(): received = lax.ppermute(far_out.reshape(HALF, 2, 128), 'c', swap)  2.14 us
    ppermute x1, starting transfers between devices, local(): received = lax.ppermute(far_out.reshape(HALF, 2, 128), 'c', swap)  2.03 us
  transfers between devices with their start and end apart: 2, of which 2 were waited for; matrix products, arithmetic and copies ran while one was open for 0% of the time, Pallas kernels for 1%

profile of v8, /device:TPU:8, one launch (start us, length us, event | category | flops | bytes accessed | tf_op | source)
XLA Modules:
  0.0 100.9 jit_solution(13642041101605439490)
XLA Ops:
  0.0 0.0 copy-start.7
  0.0 0.0 copy-start.4
  0.0 0.7 copy-done.4
  0.7 0.0 copy-start.6
  0.7 3.0 %pick_rows.1 = (s32[8,256]{1,0:T(8,128)S(1)}, s32[8,128]{1,0:T(8,128)S(1)}, bf16[192,128]{1,0:T(8,128)(2,1)S(1)}) custom-call(s32[1]{0:T(128)} %bitcast.me_ref, s32[8,256]{1,0:T(8,128)S(1)} %copy-done.4, bf16[1024,128]{1,0:T(8,128)(2,1)} %bitcast.36, s32[2048,128]{1,0:T(8,128)} %bitcast.35), custom_call_target="tpu_custom_call" | custom-call | tf_op jit(solution)/shard_map/pick_rows/pallas_call | solution.py:314
  3.7 27.0 %all_to_all.20 = bf16[16,6,2,128]{3,2,1,0:T(2,128)(2,1)S(1)} all-to-all(bf16[16,6,2,128]{3,2,1,0:T(2,128)(2,1)S(1)} %bitcast.32), channel_id=1, replica_groups=mesh['zh'=4,'c'=2,'yh'=4,'yl'=2,'x'=4,'zl'=2] {'zh','yh'}, dimensions={0} | all-to-all | bytes 98304 | tf_op jit(solution)/shard_map/all_to_all | solution.py:403
  30.7 0.6 broadcast_in_dim.8
  31.4 17.2 %all_to_all.21 = bf16[16,96,2,128]{3,2,1,0:T(2,128)(2,1)S(1)} all-to-all(bf16[16,96,2,128]{3,2,1,0:T(2,128)(2,1)S(1)} %broadcast_in_dim.8), channel_id=1, replica_groups=mesh['zh'=4,'c'=2,'yh'=4,'yl'=2,'x'=4,'zl'=2] {'x','zl','yl'}, dimensions={0} | all-to-all | bytes 1572864 | tf_op jit(solution)/shard_map/all_to_all | solution.py:405
  48.6 1.9 %collective-permute-start = (bf16[1536,2,128]{2,1,0:T(2,128)(2,1)S(1)}, bf16[1536,2,128]{2,1,0:T(2,128)(2,1)S(1)}, u32[]{:S(2)}, u32[]{:S(2)}) collective-permute-start(bf16[1536,2,128]{2,1,0:T(2,128)(2,1)S(1)} %bitcast.24), channel_id=1, source_target_pairs={{0,64},{64,0},{1,65},{65,1},{2,66},{66,2},{3,67},{67,3},{4,68},{68... | collective-permute-start | bytes 2359304 | tf_op jit(solution)/shard_map/ppermute | solution.py:407
  50.5 0.0 copy-done.7
  50.5 0.0 copy-done.6
  50.5 0.0 copy-start
  50.5 0.0 copy-start.1
  50.5 0.0 copy-start.2
  50.5 0.0 copy-start.3
  50.5 0.0 copy-start.5
  50.6 1.4 %ctf_images.1 = (f32[2048,128]{1,0:T(8,128)S(1)}, f32[1024,128]{1,0:T(8,128)S(1)}) custom-call(f32[4]{0:T(128)S(1)} %copy-done.7, bf16[2048,128]{1,0:T(8,128)(2,1)S(1)} %bitcast.34), custom_call_target="tpu_custom_call" | custom-call | flops 4000000000 | bytes 4000000 | tf_op jit(solution)/shard_map/ctf_images/pallas_call | solution.py:336
  51.9 0.8 collective-permute-done
  52.7 0.0 copy-done
  52.7 0.0 copy-done.1
  52.7 0.0 copy-done.2
  52.7 0.0 copy-done.3
  52.7 0.0 copy-done.5
  52.8 10.4 %shift_search.1 = (f32[6144,128]{1,0:T(8,128)S(1)}, bf16[3072,128]{1,0:T(8,128)(2,1)S(1)}) custom-call(s32[8,256]{1,0:T(8,128)S(1)} %get-tuple-element.13.pos_ref, f32[4]{0:T(128)S(1)} %copy-done.5, bf16[3072,128]{1,0:T(8,128)(2,1)S(1)} %bitcast.25, bf16[3072,128]{1,0:T(8,128)(2,1)S(1)} %bitcast.28, f32[2048,128]{1,0:T(8,128)S(1)} %get-tuple-element.15.img_ref, ...), custom_call_target="tpu_custom_call" | custom-call | tf_op jit(solution)/shard_map/shift_search/pallas_call | solution.py:350
  63.2 2.0 %collective-permute-start.1 = (bf16[1536,2,128]{2,1,0:T(2,128)(2,1)S(1)}, bf16[1536,2,128]{2,1,0:T(2,128)(2,1)S(1)}, u32[]{:S(2)}, u32[]{:S(2)}) collective-permute-start(bf16[1536,2,128]{2,1,0:T(2,128)(2,1)S(1)} %bitcast.33), channel_id=1, source_target_pairs={{0,64},{64,0},{1,65},{65,1},{2,66},{66,2},{3,67},{67,3},{4,68},{68... | collective-permute-start | bytes 2359304 | tf_op jit(solution)/shard_map/ppermute | solution.py:412
  65.2 2.1 %collective-permute-done.1 = bf16[1536,2,128]{2,1,0:T(2,128)(2,1)S(1)} collective-permute-done((bf16[1536,2,128]{2,1,0:T(2,128)(2,1)S(1)}, bf16[1536,2,128]{2,1,0:T(2,128)(2,1)S(1)}, u32[]{:S(2)}, u32[]{:S(2)}) %collective-permute-start.1) | collective-permute-done | bytes 786464 | tf_op jit(solution)/shard_map/ppermute | solution.py:412
  67.4 0.2 add_core.1
  67.6 16.8 %all_to_all.22 = bf16[16,96,2,128]{3,2,1,0:T(2,128)(2,1)S(1)} all-to-all(bf16[16,96,2,128]{3,2,1,0:T(2,128)(2,1)S(1)} %bitcast.26), channel_id=1, replica_groups=mesh['zh'=4,'c'=2,'yh'=4,'yl'=2,'x'=4,'zl'=2] {'x','zl','yl'}, dimensions={0} | all-to-all | bytes 1572864 | tf_op jit(solution)/shard_map/all_to_all | solution.py:414
  84.4 0.1 add_line.1
  84.5 15.0 %all_to_all.23 = bf16[16,6,2,128]{3,2,1,0:T(2,128)(2,1)S(1)} all-to-all(bf16[16,6,2,128]{3,2,1,0:T(2,128)(2,1)S(1)} %bitcast.31), channel_id=1, replica_groups=mesh['zh'=4,'c'=2,'yh'=4,'yl'=2,'x'=4,'zl'=2] {'zh','yh'}, dimensions={0} | all-to-all | bytes 98304 | tf_op jit(solution)/shard_map/all_to_all | solution.py:416
  99.5 1.4 %insert_rows.1 = f32[1024,128]{1,0:T(8,128)} custom-call(s32[8,128]{1,0:T(8,128)S(1)} %get-tuple-element.12.mine_ref, bf16[192,128]{1,0:T(8,128)(2,1)S(1)} %bitcast.30), custom_call_target="tpu_custom_call" | custom-call | tf_op jit(solution)/shard_map/insert_rows/pallas_call | solution.py:382
Async XLA Ops:
  0.0 50.5 %copy-start.7 = (f32[4]{0:T(128)S(1)}, f32[4]{0:T(128)}, u32[]{:S(2)}) copy-start(f32[4]{0:T(128)} %defocus_ref.1) | copy-start | bytes 52
  0.0 0.7 copy-start.4
  0.7 49.8 %copy-start.6 = (bf16[4,256,2,128]{3,2,1,0:T(2,128)(2,1)S(1)}, bf16[4,256,2,128]{3,2,1,0:T(2,128)(2,1)}, u32[]{:S(2)}) copy-start(bf16[4,256,2,128]{3,2,1,0:T(2,128)(2,1)} %param.10) | copy-start | bytes 1572868
  48.6 4.2 %collective-permute-start = (bf16[1536,2,128]{2,1,0:T(2,128)(2,1)S(1)}, bf16[1536,2,128]{2,1,0:T(2,128)(2,1)S(1)}, u32[]{:S(2)}, u32[]{:S(2)}) collective-permute-start(bf16[1536,2,128]{2,1,0:T(2,128)(2,1)S(1)} %bitcast.24), channel_id=1, source_target_pairs={{0,64},{64,0},{1,65},{65,1},{2,66},{66,2},{3,67},{67,3},{4,68},{68... | collective-permute-start | bytes 2359304 | tf_op jit(solution)/shard_map/ppermute | solution.py:407
  50.5 2.2 %copy-start = (bf16[256,1024]{1,0:T(8,128)(2,1)S(1)}, bf16[256,1024]{1,0:T(8,128)(2,1)}, u32[]{:S(2)}) copy-start(bf16[256,1024]{1,0:T(8,128)(2,1)} %constant.42.clone.bwd_ref) | copy-start | bytes 1572868
  50.5 2.2 %copy-start.1 = (bf16[1024,256]{1,0:T(8,128)(2,1)S(1)}, bf16[1024,256]{1,0:T(8,128)(2,1)}, u32[]{:S(2)}) copy-start(bf16[1024,256]{1,0:T(8,128)(2,1)} %constant.41.clone.fwd_ref) | copy-start | bytes 1572868
  50.5 2.2 %copy-start.2 = (bf16[512,32]{1,0:T(8,128)(2,1)S(1)}, bf16[512,32]{1,0:T(8,128)(2,1)}, u32[]{:S(2)}) copy-start(bf16[512,32]{1,0:T(8,128)(2,1)} %constant.44.clone.back_ref) | copy-start | bytes 98308
  50.5 2.2 %copy-start.3 = (bf16[64,256]{1,0:T(8,128)(2,1)S(1)}, bf16[64,256]{1,0:T(8,128)(2,1)}, u32[]{:S(2)}) copy-start(bf16[64,256]{1,0:T(8,128)(2,1)} %constant.43.clone.corr_ref) | copy-start | bytes 98308
  50.5 2.2 %copy-start.5 = (f32[4]{0:T(128)S(1)}, f32[4]{0:T(128)}, u32[]{:S(2)}) copy-start(f32[4]{0:T(128)} %noise_ref.1) | copy-start | bytes 52
  63.2 4.2 %collective-permute-start.1 = (bf16[1536,2,128]{2,1,0:T(2,128)(2,1)S(1)}, bf16[1536,2,128]{2,1,0:T(2,128)(2,1)S(1)}, u32[]{:S(2)}, u32[]{:S(2)}) collective-permute-start(bf16[1536,2,128]{2,1,0:T(2,128)(2,1)S(1)} %bitcast.33), channel_id=1, source_target_pairs={{0,64},{64,0},{1,65},{65,1},{2,66},{66,2},{3,67},{67,3},{4,68},{68... | collective-permute-start | bytes 2359304 | tf_op jit(solution)/shard_map/ppermute | solution.py:412
